TPU v7x, 32 devices: a whole 2x2x4 slice. The times are simulated.
32 devices in a mesh: grp: 2 (over y), pencil: 4 (over z), depth: 2 (over x), mem: 2 (over core).
Axes of the slice: x: 2, y: 2, z: 4, core: 2. Of those that a mesh axis runs over, the one named last changes fastest.
Arguments:
- density: float32 [4, 2, 2048, 2048], P(('grp', 'mem'), 'depth', 'pencil'), parts along dimension 0, may hold values from -6 to 6
- background: float32 [8, 2], P(None, 'depth'), may hold values from -2 to 2
- member_ids: int32 [4], P(('grp', 'mem')), parts along dimension 0, may hold values from 0 to 7
- layer_kernel: int32 [2], P('depth'), may hold values from 0 to 3, as said below
- kernel_spectra: bfloat16 [4, 2, 2048, 2048], P('depth', None, None, 'pencil'), may hold values from -4 to 4
Outputs:
- gravity: float32 [4, 2048, 2048], P(('grp', 'mem'), ('pencil', 'depth')), parts along dimension 0
There are 2 independent parts, one for each index of `grp`. A program takes and returns all parts, laid end to end along the dimension named above; an argument that names none is the same for every part. Nothing has to cross between parts.
Inputs may be any that keep to these rules, and one draw needn't show every extreme that they name: Layer l takes one of the 2 kernels of its depth band: layer_kernel[l] // 2 equals l.
All inputs are finite; a program needn't handle non-finite values.
Results may differ from a plain program's by a relative error of at most 0.0003.
Values sent between devices are 32-bit elements; how exact they have to be, the bound alone decides.
A program may use at most 128 MiB of HBM per device.

v0:
```python
import functools
import math

import jax
import jax.numpy as jnp
import numpy as np
from jax import lax
from jax.experimental import pallas as pl
from jax.experimental.pallas import tpu as pltpu
from jax.sharding import PartitionSpec as P

RADIX = 16
INNER = 128
HALF = 64
LENGTH = RADIX * INNER
f32 = jnp.float32
bf16 = jnp.bfloat16


def halves(table):
    table = np.asarray(table, np.float32)
    high = table.astype(bf16)
    low = (table - high.astype(np.float32)).astype(bf16)
    return jnp.asarray(high), jnp.asarray(low)


def residue_rows(r):
    m = np.arange(INNER)[:, None]
    q = np.arange(HALF)[None, :]
    turn = np.exp(-2j * np.pi * (((RADIX * q + r) * m) % LENGTH) / LENGTH)
    re, im = turn.real.copy(), turn.imag.copy()
    if r == 0:
        im[:, 0] = (-1.0) ** m[:, 0]
    out = np.zeros((2 * INNER, 2 * HALF))
    if r == 0:
        out[:INNER, :HALF], out[:INNER, HALF:] = re, im
    elif r == 8:
        out[INNER:, :HALF], out[INNER:, HALF:] = re, im
    else:
        sign = 1.0 if r < 8 else -1.0
        out[:INNER, :HALF], out[:INNER, HALF:] = re, im
        out[INNER:, :HALF], out[INNER:, HALF:] = -sign * im, sign * re
    return out


def slot_of(r):
    return 0 if r in (0, 8) else min(r, RADIX - r)


def row_tables():
    tables = np.zeros((8, 512, 256))
    for t in range(8):
        for odd in range(2):
            block = residue_rows(2 * t + odd)
            rows = slice(256 * odd, 256 * odd + 256)
            tables[t, rows, HALF * odd : HALF * odd + HALF] = block[:, :HALF]
            tables[t, rows, 128 + HALF * odd : 128 + HALF * odd + HALF] = block[:, HALF:]
    return tables


def inverse_row_tables():
    tables = np.zeros((8, 512, 256))
    scale = 1.0 / (LENGTH * LENGTH)
    for s in range(8):
        for place, r in enumerate((s, 8 if s == 0 else RADIX - s)):
            block = residue_rows(r).T.copy() * scale
            weight = np.full((2 * HALF, 1), 2.0 if r in (0, 8) else 1.0)
            if r == 0:
                weight[0] = weight[HALF] = 1.0
            block *= weight
            odd = r % 2
            tables[s, 256 * place + HALF * odd : 256 * place + HALF * odd + HALF] += block[:HALF]
            tables[s, 256 * place + 128 + HALF * odd : 256 * place + 128 + HALF * odd + HALF] += block[HALF:]
    return tables


def column_tables():
    q = np.arange(INNER)[:, None]
    m = np.arange(INNER)[None, :]
    turn = np.exp(-2j * np.pi * ((q * m) % INNER) / INNER)
    table = np.block([[turn.real, -turn.imag], [turn.imag, turn.real]])
    angles = 2 * np.pi * np.arange(RADIX)[:, None] * np.arange(INNER)[None, :] / LENGTH
    turns = np.zeros((RADIX, INNER, INNER), np.float32)
    turns[..., 0] = np.cos(angles)
    turns[..., 1] = np.sin(angles)
    return table, turns


def split_value(value):
    high = value.astype(bf16)
    return high, (value - high.astype(f32)).astype(bf16)


def dot(a, b):
    return jnp.dot(a, b, preferred_element_type=f32)


def rotate(value, count, length, sign):
    re, im = value
    count %= length
    if count == 0:
        return value
    if 4 * count == length:
        return (im, -re) if sign < 0 else (-im, re)
    c = math.cos(2 * math.pi * count / length)
    s = sign * math.sin(2 * math.pi * count / length)
    if 8 * count == length:
        return ((re + im) * c, (im - re) * c) if sign < 0 else ((re - im) * c, (im + re) * c)
    return (re * c - im * s, re * s + im * c)


def plus(a, b):
    return (a[0] + b[0], a[1] + b[1])


def minus(a, b):
    return (a[0] - b[0], a[1] - b[1])


def transform(values, sign):
    length = len(values)
    if length == 1:
        return values
    even, odd = transform(values[0::2], sign), transform(values[1::2], sign)
    turned = [rotate(odd[k], k, length, sign) for k in range(length // 2)]
    return [plus(even[k], turned[k]) for k in range(length // 2)] + [
        minus(even[k], turned[k]) for k in range(length // 2)
    ]


def real_transform(values):
    length = len(values)
    if length == 2:
        return [(values[0] + values[1], None), (values[0] - values[1], None)]
    even, odd = real_transform(values[0::2]), real_transform(values[1::2])
    out = [None] * (length // 2 + 1)
    out[0] = (even[0][0] + odd[0][0], None)
    out[length // 2] = (even[0][0] - odd[0][0], None)
    quarter = length // 4
    for k in range(1, quarter):
        turned = rotate(odd[k], k, length, -1)
        out[k] = plus(even[k], turned)
        low = minus(even[k], turned)
        out[length // 2 - k] = (low[0], -low[1])
    out[quarter] = (even[quarter][0], -odd[quarter][0])
    return out


def real_inverse(values):
    half = len(values) - 1
    length = 2 * half
    if length == 2:
        return [values[0][0] + values[1][0], values[0][0] - values[1][0]]
    even, odd = [], []
    for k in range(half // 2 + 1):
        if k == 0:
            even.append((values[0][0] + values[half][0], None))
            odd.append((values[0][0] - values[half][0], None))
        elif k == half // 2:
            even.append((2.0 * values[k][0], None))
            odd.append((-2.0 * values[k][1], None))
        else:
            other = values[half - k]
            even.append((values[k][0] + other[0], values[k][1] - other[1]))
            odd.append(rotate((values[k][0] - other[0], values[k][1] + other[1]), k, length, 1))
    first, second = real_inverse(even), real_inverse(odd)
    return [x for pair in zip(first, second) for x in pair]


def rows_kernel(pencils, width, offset_ref, in_ref, high_ref, low_ref, *rest):
    outs, pieces = rest[:-1], rest[-1]
    rows = in_ref.shape[0]
    per = RADIX // pencils
    offset = offset_ref[0]

    def step(b, carry):
        at = pl.ds(pl.multiple_of(b * 8, 8), 8)
        values = [in_ref[at, n * INNER : (n + 1) * INNER] - offset for n in range(RADIX)]
        got = real_transform(values)
        pieces[0, at, :INNER] = got[0][0]
        pieces[0, at, INNER:] = got[8][0]
        for s in range(1, 8):
            pieces[s, at, :INNER] = got[s][0]
            pieces[s, at, INNER:] = got[s][1]
        return carry

    lax.fori_loop(0, rows // 8, step, 0)
    for t in range(8):
        total = None
        for odd in range(2):
            high, low = split_value(pieces[slot_of(2 * t + odd)])
            table_high = high_ref[t, 256 * odd : 256 * odd + 256]
            table_low = low_ref[t, 256 * odd : 256 * odd + 256]
            part = dot(high, table_high) + dot(low, table_high) + dot(high, table_low)
            total = part if total is None else total + part
        if width == 2:
            pencil, place = divmod(2 * t, per)
            for c in range(2):
                outs[place // 2][pencil, c] = total[:, c * 128 : (c + 1) * 128]
        else:
            for odd in range(2):
                pencil, place = divmod(2 * t + odd, per)
                for c in range(2):
                    begin = c * 128 + odd * HALF
                    outs[place][pencil, c] = total[:, begin : begin + HALF]


def swapped(zero, shape, axis):
    total = lax.broadcasted_iota(jnp.int32, shape, 0) + lax.broadcasted_iota(jnp.int32, shape, 1)
    wanted = jnp.where(zero, INNER, INNER - 1)
    also = jnp.where(zero, 0, INNER - 1)
    return jnp.where((total == wanted) | (total == also), 1.0, 0.0).astype(bf16)


def mirror_kernel(share, where_ref, *refs):
    ins, zero_ref, rest_refs = refs[:share], refs[share], refs[share + 1 :]
    per = ins[0].shape[2] // INNER
    plain = swapped(where_ref[1] < 0, (INNER, HALF), 1)
    edge = swapped(where_ref[2] == 0, (INNER, HALF), 1)
    for u in range(share):
        swap = swapped(where_ref[1] + u == 0, (INNER, INNER), 0)
        rows = [dot(swap, ins[u][c]).astype(bf16) for c in range(2)]
        for j in range(per):
            turn = edge if j == 0 else plain
            turned = [dot(rows[c][:, j * INNER : (j + 1) * INNER], turn) for c in range(2)]
            value = jnp.concatenate(turned, axis=1)
            if j == 0:
                zero_ref[0, u] = value
            else:
                rest_refs[0][per - 1 - j, u] = value


def columns_kernel(special, where_ref, in_ref, kern_ref, mirror_ref, edge_ref,
                   turns_ref, late_ref, table_ref, out_ref, pieces, waves):
    part_rows = in_ref.shape[2]
    depths, pencils, _, out_rows, lanes = out_ref.shape
    share = mirror_ref.shape[1]
    steps = RADIX // share
    mine = where_ref[0]
    now = pl.program_id(0)
    from_lane = lax.broadcasted_iota(jnp.int32, (kern_ref.shape[2], lanes), 0)
    to_lane = lax.broadcasted_iota(jnp.int32, (kern_ref.shape[2], lanes), 1)
    wanted = to_lane + jnp.where(to_lane < HALF, 0, HALF)
    pick = jnp.where(from_lane == wanted, 0.5, 0.0).astype(bf16)
    zero_swap = swapped(mine >= 0, (INNER, INNER), 0)
    plain_swap = swapped(mine < 0, (INNER, INNER), 0)

    def forward(b, carry):
        values = []
        for n in range(RADIX):
            source, begin = divmod(n * INNER, part_rows)
            at = pl.ds(pl.multiple_of(begin + b * 8, 8), 8)
            values.append((in_ref[source, 0, at, :], in_ref[source, 1, at, :]))
        at = pl.ds(pl.multiple_of(b * 8, 8), 8)
        also = pl.ds(pl.multiple_of(INNER + b * 8, 8), 8)
        for r, (re, im) in enumerate(transform(values, -1)):
            pieces[r, at, :] = re
            pieces[r, also, :] = im
        return carry

    @pl.when(now == 0)
    def _():
        lax.fori_loop(0, INNER // 8, forward, 0)

    def wave(r, u):
        re, im = pieces[r, :INNER], pieces[r, INNER:]
        c, s = turns_ref[u, :, 0:1], turns_ref[u, :, 1:2]
        high, low = split_value(jnp.concatenate([re * c + im * s, im * c - re * s], axis=0))
        return dot(table_ref[0], high) + dot(table_ref[0], low) + dot(table_ref[1], high)

    def finish(r, u, got):
        re, im = got[:INNER], got[INNER:]
        tiles = [mirror_ref[j, u] for j in range(mirror_ref.shape[0])]
        rows = slice(u * INNER, (u + 1) * INNER)
        parts = []
        for c in range(2):
            other = [tile[:, c * HALF : (c + 1) * HALF] for tile in tiles]
            other = jnp.concatenate(other, axis=1) if len(other) > 1 else other[0]
            own = dot(kern_ref[c, rows, :], pick)
            parts.append(own + 0.5 * other if c == 0 else own - 0.5 * other)
        kr, ki = parts
        if special:
            other = lax.rem(RADIX - r, RADIX)
            high, low = split_value(waves[other])
            swap = jnp.where(r == 0, zero_swap.astype(f32), plain_swap.astype(f32)).astype(bf16) if u == 0 else plain_swap
            ore = dot(swap, high[:INNER]) + dot(swap, low[:INNER])
            oim = -(dot(swap, high[INNER:]) + dot(swap, low[INNER:]))
            mask = (lax.broadcasted_iota(jnp.int32, (INNER, lanes), 1) == 0) & (where_ref[2] == 0)
            hr = jnp.where(mask, 0.5 * (kr - edge_ref[0, u]), 0.0)
            hi = jnp.where(mask, 0.5 * (ki - edge_ref[1, u]), 0.0)
            kr, ki = kr - hr, ki - hi
            sr = re * kr - im * ki + (ore * hr - oim * hi)
            si = re * ki + im * kr + (ore * hi + oim * hr)
        else:
            sr, si = re * kr - im * ki, re * ki + im * kr
        spectrum = jnp.concatenate([sr, si], axis=0)
        high, low = split_value(spectrum)
        got = dot(table_ref[2], high) + dot(table_ref[2], low) + dot(table_ref[3], high)
        re, im = got[:INNER], got[INNER:]
        c, s = late_ref[u, :, 0:1], late_ref[u, :, 1:2]
        pieces[r, :INNER] = re * c - im * s
        pieces[r, INNER:] = im * c + re * s

    if special:
        @pl.when(now < steps)
        def _():
            for u in range(share):
                waves[now * share + u] = wave(now * share + u, u)

        @pl.when(now >= steps)
        def _():
            for u in range(share):
                r = (now - steps) * share + u
                finish(r, u, waves[r])
    else:
        for u in range(share):
            r = now * share + u
            finish(r, u, wave(r, u))

    slots = [lax.rem(d - mine + depths, depths) for d in range(depths)]

    def backward(b, carry):
        at = pl.ds(pl.multiple_of(b * 8, 8), 8)
        also = pl.ds(pl.multiple_of(INNER + b * 8, 8), 8)
        values = [(pieces[r, at, :], pieces[r, also, :]) for r in range(RADIX)]
        for n, (re, im) in enumerate(transform(values, 1)):
            if out_rows % INNER == 0:
                part, begin = divmod(n * INNER, out_rows)
                pencil, depth = divmod(part, depths)
                depth = slots[depth]
                put = pl.ds(pl.multiple_of(begin + b * 8, 8), 8)
            else:
                x = n * INNER + b * 8
                pencil = x // (out_rows * depths)
                depth = lax.rem(x // out_rows - mine + depths, depths)
                put = pl.ds(pl.multiple_of(lax.rem(x, out_rows), 8), 8)
            out_ref[depth, pencil, 0, put, :] = re
            out_ref[depth, pencil, 1, put, :] = im
        return carry

    @pl.when(now == pl.num_programs(0) - 1)
    def _():
        lax.fori_loop(0, INNER // 8, backward, 0)


def fields_kernel(pencils, width, counts, *refs):
    ins, at = [], 0
    for count in counts:
        ins.append(refs[at : at + count])
        at += count
    high_ref, low_ref, out_ref, pieces = refs[at:]
    per = RADIX // pencils
    rows = out_ref.shape[1]

    def read(chunk, pencil, c):
        found = [ref[pencil, c] for ref in ins[chunk]]
        return jnp.concatenate(found, axis=0) if len(found) > 1 else found[0]

    def pair(t):
        if width == 2:
            pencil, place = divmod(2 * t, per)
            return jnp.concatenate([read(place // 2, pencil, c) for c in range(2)], axis=1)
        found = []
        for c in range(2):
            for odd in range(2):
                pencil, place = divmod(2 * t + odd, per)
                found.append(read(place, pencil, c))
        return jnp.concatenate(found, axis=1)

    for s in range(8):
        total = None
        for place, r in enumerate((s, 8 if s == 0 else RADIX - s)):
            high, low = split_value(pair(r // 2))
            table_high = high_ref[s, 256 * place : 256 * place + 256]
            table_low = low_ref[s, 256 * place : 256 * place + 256]
            part = dot(high, table_high) + dot(low, table_high) + dot(high, table_low)
            total = part if total is None else total + part
        pieces[s] = total

    def step(b, carry):
        at = pl.ds(pl.multiple_of(b * 8, 8), 8)
        values = [(pieces[0, at, :INNER], None)]
        for s in range(1, 8):
            values.append((pieces[s, at, :INNER], pieces[s, at, INNER:]))
        values.append((pieces[0, at, INNER:], None))
        for n, value in enumerate(real_inverse(values)):
            out_ref[0, at, n * INNER : (n + 1) * INNER] = value
        return carry

    lax.fori_loop(0, rows // 8, step, 0)


def params(**more):
    return pltpu.CompilerParams(vmem_limit_bytes=48 * 1024 * 1024, **more)


def body(density, background, member_ids, layer_kernel, kernel_spectra):
    pencils = lax.axis_size("pencil")
    depths = lax.axis_size("depth")
    sharers = lax.axis_size("grp") * lax.axis_size("mem")
    pencil = lax.axis_index("pencil")
    per = RADIX // pencils
    width = min(per, 2)
    chunks = per // width
    lanes = width * HALF
    part_rows = density.shape[2]
    out_rows = part_rows // depths
    vmem = pl.BlockSpec(memory_space=pltpu.VMEM)
    smem = pl.BlockSpec(memory_space=pltpu.SMEM)

    kern_count = kernel_spectra.shape[0]
    local = layer_kernel[0] - lax.axis_index("depth") * kern_count
    share = RADIX // sharers
    first = lax.axis_index(("grp", "mem")) * share
    groups = [1] if per == 1 else [1, per - 1]
    moved = pl.pallas_call(
        functools.partial(mirror_kernel, share),
        grid_spec=pltpu.PrefetchScalarGridSpec(
            num_scalar_prefetch=1,
            grid=(1,),
            in_specs=[
                pl.BlockSpec(
                    (None, 2, INNER, per * INNER),
                    lambda i, w, u=u: (w[0], 0, lax.rem(RADIX - w[1] - u, RADIX), 0),
                )
                for u in range(share)
            ],
            out_specs=[pl.BlockSpec((g, share, INNER, INNER), lambda i, w: (0, 0, 0, 0)) for g in groups],
        ),
        out_shape=[jax.ShapeDtypeStruct((g, share, INNER, INNER), f32) for g in groups],
        compiler_params=params(),
        cost_estimate=pl.CostEstimate(flops=1 << 20, bytes_accessed=2 << 20, transcendentals=0),
    )(jnp.stack([local, first, pencil]), *[kernel_spectra] * share)
    mirrored = lax.ppermute(moved[0], "pencil", [(p, (pencils - p) % pencils) for p in range(pencils)])
    if per > 1:
        rest = lax.ppermute(moved[1], "pencil", [(p, pencils - 1 - p) for p in range(pencils)])

    offset = lax.dynamic_index_in_dim(background[:, 0], member_ids[0], 0, keepdims=True)
    row_high, row_low = halves(row_tables())
    block = min(part_rows, 128)
    sent = pl.pallas_call(
        functools.partial(rows_kernel, pencils, width),
        grid=(part_rows // block,),
        in_specs=[
            smem,
            pl.BlockSpec((None, None, block, LENGTH), lambda i: (0, 0, i, 0)),
            pl.BlockSpec((8, 512, 256), lambda i: (0, 0, 0)),
            pl.BlockSpec((8, 512, 256), lambda i: (0, 0, 0)),
        ],
        out_specs=[pl.BlockSpec((pencils, 2, block, lanes), lambda i: (0, 0, i, 0))] * chunks,
        out_shape=[jax.ShapeDtypeStruct((pencils, 2, part_rows, lanes), f32)] * chunks,
        scratch_shapes=[pltpu.VMEM((8, block, 256), f32)],
        compiler_params=params(),
        cost_estimate=pl.CostEstimate(flops=6 * part_rows * 2 * LENGTH * 512, bytes_accessed=12 << 20, transcendentals=0),
    )(offset, density, row_high, row_low)
    arrived = [lax.all_to_all(part, "pencil", 0, 0, tiled=True) for part in sent]

    sign = jnp.array([0.5, -0.5], f32)
    edge = lax.dynamic_slice(kernel_spectra, (local, 0, 0, HALF), (1, 2, LENGTH, 1))
    edge = edge.reshape(2, RADIX, INNER).astype(f32)
    flipped = jnp.concatenate([edge[:, :1], edge[:, :0:-1]], axis=1)[..., ::-1]
    flipped = jnp.concatenate([jnp.roll(flipped[:, :1], 1, axis=2), flipped[:, 1:]], axis=1)
    edge = 0.5 * edge + sign.reshape(2, 1, 1) * flipped
    edge = jnp.where(lax.broadcasted_iota(jnp.int32, (lanes,), 0) == 0, edge[..., None], 0.0)

    if per > 1:
        mirrored = jnp.concatenate([mirrored, rest], axis=0)
    mirrored, edge, _ = lax.optimization_barrier((mirrored, edge, sent[0]))
    mirrored = lax.all_gather(mirrored, ("grp", "mem"), axis=0)

    column, column_turns = column_tables()
    column_turns = jnp.asarray(column_turns)
    tables = jnp.stack(halves(column) + halves(column.T))
    two = depths == 2
    mine = lax.axis_index("depth") if two else jnp.int32(0)
    where = jnp.stack([mine, local, pencil])
    fields = []
    before = None
    for k in range(chunks):
        special = k == 0
        steps = sharers

        def early(i, special=special):
            return jnp.minimum(i, steps - 1) if special else i

        def late(i, special=special):
            return jnp.maximum(i - steps, 0) if special else i

        here = arrived[k]
        if before is not None:
            here, before = lax.optimization_barrier((here, before))
            fields.append(lax.all_to_all(before, "pencil", 0, 0, tiled=True))
        edge_block = (2, share, INNER, lanes) if special else (2, 1, 8, lanes)
        out = pl.pallas_call(
            functools.partial(columns_kernel, special),
            grid_spec=pltpu.PrefetchScalarGridSpec(
                num_scalar_prefetch=1,
                grid=(2 * steps if special else steps,),
                in_specs=[
                    pl.BlockSpec((pencils, 2, part_rows, lanes), lambda i, w: (0, 0, 0, 0)),
                    pl.BlockSpec(
                        (None, 2, share * INNER, width * INNER), lambda i, w, k=k, late=late: (w[1], 0, late(i), k)
                    ),
                    pl.BlockSpec(
                        (None, width, share, INNER, INNER), lambda i, w, k=k, late=late: (late(i), k, 0, 0, 0)
                    ),
                    pl.BlockSpec(
                        edge_block,
                        (lambda i, w, late=late: (0, late(i), 0, 0)) if special else (lambda i, w: (0, 0, 0, 0)),
                    ),
                ]
                + [pl.BlockSpec((share, INNER, INNER), lambda i, w, early=early: (early(i), 0, 0))]
                + [pl.BlockSpec((share, INNER, INNER), lambda i, w, late=late: (late(i), 0, 0))]
                + [pl.BlockSpec((4, 256, 256), lambda i, w: (0, 0, 0))],
                out_specs=pl.BlockSpec((depths, pencils, 2, out_rows, lanes), lambda i, w: (0, 0, 0, 0, 0)),
                scratch_shapes=[
                    pltpu.VMEM((RADIX, 256, lanes), f32),
                    pltpu.VMEM((RADIX if special else 1, 256, lanes), f32),
                ],
            ),
            out_shape=jax.ShapeDtypeStruct((depths, pencils, 2, out_rows, lanes), f32),
            compiler_params=params(),
            cost_estimate=pl.CostEstimate(
                flops=12 * RADIX * 256 * 256 * lanes, bytes_accessed=16 << 20, transcendentals=0
            ),
        )(where, here, kernel_spectra, mirrored, edge, column_turns, column_turns, tables)
        if two:
            before = out[0] + lax.ppermute(out[1], "depth", [(0, 1), (1, 0)])
        else:
            before = lax.psum_scatter(out, "depth", scatter_dimension=0, tiled=False)
    fields.append(lax.all_to_all(before, "pencil", 0, 0, tiled=True))

    back_high, back_low = halves(inverse_row_tables())
    return pl.pallas_call(
        functools.partial(fields_kernel, pencils, width, [1] * chunks),
        in_specs=[vmem] * (len(fields) + 2),
        out_specs=vmem,
        out_shape=jax.ShapeDtypeStruct((1, out_rows, LENGTH), f32),
        scratch_shapes=[pltpu.VMEM((8, out_rows, 256), f32)],
        compiler_params=params(),
        cost_estimate=pl.CostEstimate(flops=6 * out_rows * 2 * LENGTH * 512, bytes_accessed=8 << 20, transcendentals=0),
    )(*fields, back_high, back_low)


def solution(mesh):
    placed = (
        P(("grp", "mem"), "depth", "pencil", None),
        P(None, "depth"),
        P(("grp", "mem")),
        P("depth"),
        P("depth", None, None, "pencil"),
    )
    return jax.shard_map(
        body,
        mesh=mesh,
        in_specs=placed,
        out_specs=P(("grp", "mem"), ("pencil", "depth"), None),
        check_vma=False,
    )
```

profile of v0, /device:TPU:18, one launch (start us, length us, event | category | flops | bytes accessed | tf_op | source)
XLA Modules:
  0.0 236.3 jit_solution(16438916901628065476)
XLA Ops:
  6.5 0.0 copy-start
  6.5 0.0 all-gather.3.cloned.1.call-start
  7.2 0.1 add_add_fusion.1.where_ref
  7.3 0.0 copy-start.7
  7.3 2.8 %shard_map.146 = (f32[1,4,128,128]{3,2,1,0:T(8,128)S(1)}, f32[3,4,128,128]{3,2,1,0:T(8,128)S(1)}) custom-call(s32[3]{0:T(128)S(1)} %add_add_fusion.1.where_ref, bf16[2,2,2048,512]{3,2,1,0:T(8,128)(2,1)} %kern_ref.3, bf16[2,2,2048,512]{3,2,1,0:T(8,128)(2,1)} %kern_ref.3, bf16[2,2,2048,512]{3,2,1,0:T(8,128)(2,1)} %kern_ref.3, bf16[2,2,2048,512]{3,2,1,0:T(8,128)(2,1)} %kern_ref.3), custom_call_target="tpu_custom_call" | custom-call | flops 1048576 | bytes 2097152 | tf_op jit(solution)/shard_map/pallas_call | solution.py:416
  10.1 0.5 collective-permute-start.1
  10.6 0.7 collective-permute-start
  11.3 2.0 convert_reduce_fusion
  13.3 0.1 slice.46
  14.0 0.1 slice.40
  14.1 0.1 slice.38
  14.2 0.0 copy-done
  14.2 0.6 constant_dynamic-slice_fusion
  14.8 0.0 copy-done.7
  14.8 0.1 fusion.2
  14.9 8.7 %shard_map.145 = (f32[4,2,512,128]{3,2,1,0:T(8,128)S(1)}, f32[4,2,512,128]{3,2,1,0:T(8,128)S(1)}) custom-call(f32[1]{0:T(128)} %bitcast.1.offset_ref, f32[1,1,512,2048]{3,2,1,0:T(8,128)} %in_ref.1, bf16[8,512,256]{2,1,0:T(8,128)(2,1)} %constant.54.clone.high_ref, bf16[8,512,256]{2,1,0:T(8,128)(2,1)} %constant.55.clone.low_ref), custom_call_target="tpu_custom_call" | custom-call | flops 6442450944 | bytes 12582912 | tf_op jit(solution)/shard_map/pallas_call | solution.py:441
  23.6 0.0 copy-start.5
  23.6 1.4 copy-done.5
  25.0 1.9 broadcast_select_fusion.edge_ref
  26.9 0.0 collective-permute-done
  26.9 23.0 %collective-permute-done.1 = f32[3,4,128,128]{3,2,1,0:T(8,128)} collective-permute-done((f32[3,4,128,128]{3,2,1,0:T(8,128)S(1)}, f32[3,4,128,128]{3,2,1,0:T(8,128)}, u32[]{:S(2)}, u32[]{:S(2)}) %collective-permute-start.1) | collective-permute-done | bytes 786464 | tf_op jit(solution)/shard_map/ppermute | solution.py:436
  49.9 2.3 pad_maximum_fusion
  52.2 0.0 all-gather.3.cloned.1.call-update
  52.3 51.7 %all_to_all.20.in_ref = f32[4,2,512,128]{3,2,1,0:T(8,128)} all-to-all(f32[4,2,512,128]{3,2,1,0:T(8,128)S(1)} %get-tuple-element.14), channel_id=1, replica_groups=mesh['grp'=2,'pencil'=4,'depth'=2,'mem'=2] {'pencil'}, dimensions={0} | all-to-all | bytes 4194304 | tf_op jit(solution)/shard_map/all_to_all | solution.py:456
  103.9 0.0 copy-start.1
  103.9 6.4 %all-to-all-start = ((f32[4,2,512,128]{3,2,1,0:T(8,128)}), f32[4,2,512,128]{3,2,1,0:T(8,128)S(1)}, u32[]{:S(2)}, u32[]{:S(2)}) async-start(f32[4,2,512,128]{3,2,1,0:T(8,128)} %copy-done.5), calls=%async_computation | async-start | bytes 4194304 | tf_op jit(solution)/shard_map/all_to_all | solution.py:456
  110.3 0.1 add_add_fusion.where_ref
  110.4 0.0 all-gather.3.cloned.1.call-done
  110.4 0.0 copy-done.1
  110.4 0.0 copy-start.2
  110.4 1.6 copy-done.2
  112.0 0.0 copy-start.3
  112.0 1.0 copy-done.3
  113.1 12.9 %shard_map.147 = f32[2,4,2,256,128]{4,3,2,1,0:T(8,128)S(1)} custom-call(s32[3]{0:T(128)S(1)} %add_add_fusion.where_ref, f32[4,2,512,128]{3,2,1,0:T(8,128)S(1)} %copy-done.2, bf16[2,2,2048,512]{3,2,1,0:T(8,128)(2,1)} %kern_ref.3, f32[4,4,4,128,128]{4,3,2,1,0:T(8,128)} %bitcast.30, f32[2,16,128,128]{3,2,1,0:T(8,128)} %broadcast_select_fusion.edge_ref, ...), custom_call_target="tpu_custom_call" | custom-call | flops 1610612736 | bytes 16777216 | tf_op jit(solution)/shard_map/pallas_call | solution.py:494
  126.0 0.1 slice_bitcast_fusion.2
  126.1 0.6 collective-permute-start.2
  126.6 22.9 %collective-permute-done.2 = f32[4,2,256,128]{3,2,1,0:T(8,128)S(1)} collective-permute-done((f32[4,2,256,128]{3,2,1,0:T(8,128)S(1)}, f32[4,2,256,128]{3,2,1,0:T(8,128)S(1)}, u32[]{:S(2)}, u32[]{:S(2)}) %collective-permute-start.2) | collective-permute-done | bytes 1048608 | tf_op jit(solution)/shard_map/ppermute | solution.py:528
  149.5 1.1 fusion.1
  150.6 3.7 %all-to-all-done.in_ref = f32[4,2,512,128]{3,2,1,0:T(8,128)S(1)} async-done(((f32[4,2,512,128]{3,2,1,0:T(8,128)}), f32[4,2,512,128]{3,2,1,0:T(8,128)S(1)}, u32[]{:S(2)}, u32[]{:S(2)}) %all-to-all-start) | async-done | bytes 2097184 | tf_op jit(solution)/shard_map/all_to_all | solution.py:456
  154.3 7.5 %all-to-all-start.2 = ((f32[4,2,256,128]{3,2,1,0:T(8,128)}), f32[4,2,256,128]{3,2,1,0:T(8,128)}, u32[]{:S(2)}, u32[]{:S(2)}) async-start(f32[4,2,256,128]{3,2,1,0:T(8,128)} %fusion.1), calls=%async_computation.2 | async-start | bytes 2097152 | tf_op jit(solution)/shard_map/all_to_all | solution.py:492
  161.8 0.0 copy-start.4
  161.8 1.0 copy-done.4
  162.9 10.9 %shard_map.148 = f32[2,4,2,256,128]{4,3,2,1,0:T(8,128)S(1)} custom-call(s32[3]{0:T(128)S(1)} %add_add_fusion.where_ref, f32[4,2,512,128]{3,2,1,0:T(8,128)S(1)} %all-to-all-done.in_ref, bf16[2,2,2048,512]{3,2,1,0:T(8,128)(2,1)} %kern_ref.3, f32[4,4,4,128,128]{4,3,2,1,0:T(8,128)} %bitcast.31, f32[2,16,128,128]{3,2,1,0:T(8,128)} %broadcast_select_fusion.edge_ref, ...), custom_call_target="tpu_custom_call" | custom-call | flops 1610612736 | bytes 16777216 | tf_op jit(solution)/shard_map/pallas_call | solution.py:494
  173.7 0.1 slice_bitcast_fusion
  173.8 0.0 copy-start.6
  173.8 0.6 collective-permute-start.3
  174.4 23.3 %collective-permute-done.3 = f32[4,2,256,128]{3,2,1,0:T(8,128)S(1)} collective-permute-done((f32[4,2,256,128]{3,2,1,0:T(8,128)S(1)}, f32[4,2,256,128]{3,2,1,0:T(8,128)S(1)}, u32[]{:S(2)}, u32[]{:S(2)}) %collective-permute-start.3) | collective-permute-done | bytes 1048608 | tf_op jit(solution)/shard_map/ppermute | solution.py:528
  197.7 0.1 fusion
  197.8 0.0 all-to-all-done.2.refs_0_
  197.9 25.9 %all_to_all.21.refs_1_ = f32[4,2,256,128]{3,2,1,0:T(8,128)S(1)} all-to-all(f32[4,2,256,128]{3,2,1,0:T(8,128)S(1)} %fusion), channel_id=1, replica_groups=mesh['grp'=2,'pencil'=4,'depth'=2,'mem'=2] {'pencil'}, dimensions={0} | all-to-all | bytes 2097152 | tf_op jit(solution)/shard_map/all_to_all | solution.py:531
  223.8 0.0 copy-done.6
  223.8 5.7 %shard_map.149 = f32[1,256,2048]{2,1,0:T(8,128)} custom-call(f32[4,2,256,128]{3,2,1,0:T(8,128)} %all-to-all-done.2.refs_0_, f32[4,2,256,128]{3,2,1,0:T(8,128)S(1)} %all_to_all.21.refs_1_, bf16[8,512,256]{2,1,0:T(8,128)(2,1)S(1)} %copy-done.6, bf16[8,512,256]{2,1,0:T(8,128)(2,1)} %constant.63.clone.refs_3_), custom_call_target="tpu_custom_call" | custom-call | flops 3221225472 | bytes 8388608 | tf_op jit(solution)/shard_map/pallas_call | solution.py:534
  (4 shorter events, 0.0 us)
Async XLA Ops:
  6.5 7.7 %copy-start = (f32[8,1]{0,1:T(1,128)S(1)}, f32[8,1]{0,1:T(1,128)}, u32[]{:S(2)}) copy-start(f32[8,1]{0,1:T(1,128)} %param.16) | copy-start | bytes 100
  6.5 103.9 %all-gather.3.cloned.1.call-start = ((), (), s32[]{:S(2)}) async-start(), calls=%async_computation.4 | async-start | bytes 5242880 | tf_op jit(solution)/shard_map/all_gather | solution.py:469
  7.3 7.5 %copy-start.7 = (f32[2]{0:T(128)S(1)}, f32[2]{0:T(128)}, u32[]{:S(2)}) copy-start(f32[2]{0:T(128)} %constant.56.clone) | copy-start | bytes 28
  10.1 39.8 %collective-permute-start.1 = (f32[3,4,128,128]{3,2,1,0:T(8,128)S(1)}, f32[3,4,128,128]{3,2,1,0:T(8,128)}, u32[]{:S(2)}, u32[]{:S(2)}) collective-permute-start(f32[3,4,128,128]{3,2,1,0:T(8,128)S(1)} %get-tuple-element.16), channel_id=1, source_target_pairs={{0,12},{4,8},{8,4},{12,0},{1,13},{5,9},{9,5},{13,1},{2,14},{6,10},... | collective-permute-start | bytes 2359304 | tf_op jit(solution)/shard_map/ppermute | solution.py:436
  10.6 16.3 %collective-permute-start = (f32[1,4,128,128]{3,2,1,0:T(8,128)S(1)}, f32[1,4,128,128]{3,2,1,0:T(8,128)S(1)}, u32[]{:S(2)}, u32[]{:S(2)}) collective-permute-start(f32[1,4,128,128]{3,2,1,0:T(8,128)S(1)} %get-tuple-element.15), channel_id=1, source_target_pairs={{0,0},{4,12},{8,8},{12,4},{1,1},{5,13},{9,9},{13,5},{2,2},{6,14},{... | collective-permute-start | bytes 786440 | tf_op jit(solution)/shard_map/ppermute | solution.py:434
  23.6 1.4 copy-start.5
  103.9 6.5 %copy-start.1 = (f32[16,128,128]{2,1,0:T(8,128)S(1)}, f32[16,128,128]{2,1,0:T(8,128)}, u32[]{:S(2)}) copy-start(f32[16,128,128]{2,1,0:T(8,128)} %constant.57.clone.turns_ref.late_ref) | copy-start | bytes 3145732
  103.9 50.4 %all-to-all-start = ((f32[4,2,512,128]{3,2,1,0:T(8,128)}), f32[4,2,512,128]{3,2,1,0:T(8,128)S(1)}, u32[]{:S(2)}, u32[]{:S(2)}) async-start(f32[4,2,512,128]{3,2,1,0:T(8,128)} %copy-done.5), calls=%async_computation | async-start | bytes 4194304 | tf_op jit(solution)/shard_map/all_to_all | solution.py:456
  110.4 1.6 copy-start.2
  112.0 1.0 copy-start.3
  126.1 23.5 %collective-permute-start.2 = (f32[4,2,256,128]{3,2,1,0:T(8,128)S(1)}, f32[4,2,256,128]{3,2,1,0:T(8,128)S(1)}, u32[]{:S(2)}, u32[]{:S(2)}) collective-permute-start(f32[4,2,256,128]{3,2,1,0:T(8,128)S(1)} %slice_bitcast_fusion.2), channel_id=1, source_target_pairs={{0,2},{2,0},{1,3},{3,1},{4,6},{6,4},{5,7},{7,5},{8,10},{10,8},{9,1... | collective-permute-start | bytes 3145736 | tf_op jit(solution)/shard_map/ppermute | solution.py:528
  154.3 43.5 %all-to-all-start.2 = ((f32[4,2,256,128]{3,2,1,0:T(8,128)}), f32[4,2,256,128]{3,2,1,0:T(8,128)}, u32[]{:S(2)}, u32[]{:S(2)}) async-start(f32[4,2,256,128]{3,2,1,0:T(8,128)} %fusion.1), calls=%async_computation.2 | async-start | bytes 2097152 | tf_op jit(solution)/shard_map/all_to_all | solution.py:492
  161.8 1.0 copy-start.4
  173.8 50.0 %copy-start.6 = (bf16[8,512,256]{2,1,0:T(8,128)(2,1)S(1)}, bf16[8,512,256]{2,1,0:T(8,128)(2,1)}, u32[]{:S(2)}) copy-start(bf16[8,512,256]{2,1,0:T(8,128)(2,1)} %constant.62.clone.refs_2_) | copy-start | bytes 6291460
  173.8 23.9 %collective-permute-start.3 = (f32[4,2,256,128]{3,2,1,0:T(8,128)S(1)}, f32[4,2,256,128]{3,2,1,0:T(8,128)S(1)}, u32[]{:S(2)}, u32[]{:S(2)}) collective-permute-start(f32[4,2,256,128]{3,2,1,0:T(8,128)S(1)} %slice_bitcast_fusion), channel_id=1, source_target_pairs={{0,2},{2,0},{1,3},{3,1},{4,6},{6,4},{5,7},{7,5},{8,10},{10,8},{9,1... | collective-permute-start | bytes 3145736 | tf_op jit(solution)/shard_map/ppermute | solution.py:528
Sparse Core Ops, SparseCore 0:
  52.4 37.4 all-gather.2
where the time goes:
time: 241 us; the launch traced here: 236 us
  blocking collectives  77.6 us (32%)
  waiting for transfers between devices  73 us (30%)
  Pallas kernels  41 us (17%)
  starting transfers between devices  16.2 us (7%)
  between operations  14.8 us (6%)
  other arithmetic  7.62 us (3%)
  local copies, waits for them, and re-layouts  6.04 us (3%)
    all_to_all x1, blocking collectives, body(): lax.all_to_all(part, 'pencil', 0, 0, tiled=True)  51.7 us
    ppermute x2, waiting for transfers between devices, body(): before = out[0] + lax.ppermute(out[1], 'depth', [(0, 1), (1, 0)])  46.2 us
    all_to_all x1, blocking collectives, body(): fields.append(lax.all_to_all(before, 'pencil', 0, 0, tiled=True))  25.9 us
    pallas_call x2, Pallas kernels, body(): pl.pallas_call(functools.partial(columns_kernel, special), grid_spec=pltp...  23.8 us
    ppermute x1, waiting for transfers between devices, body(): lax.ppermute(moved[1], 'pencil', [(p, pencils - 1 - p) for p in range(pen...  23 us
    pallas_call x1, Pallas kernels, body(): pl.pallas_call(functools.partial(rows_kernel, pencils, width), grid=(part...  8.69 us
    all_to_all x1, starting transfers between devices, body(): fields.append(lax.all_to_all(before, 'pencil', 0, 0, tiled=True))  7.48 us
    all_to_all x1, starting transfers between devices, body(): lax.all_to_all(part, 'pencil', 0, 0, tiled=True)  6.42 us
  transfers between devices with their start and end apart: 7, of which 4 were waited for; matrix products, arithmetic and copies ran while one was open for 3% of the time, Pallas kernels for 14%

commit v1 on v0

--- a/solution.py
+++ b/solution.py
@@ -390,11 +390,194 @@
     lax.fori_loop(0, rows // 8, step, 0)
 
 
+def slot_at(r):
+    return jnp.where(r == 8, 0, jnp.minimum(r, RADIX - r))
+
+
+def shift_rows_kernel(pencils, offset_ref, where_ref, in_ref, high_ref, low_ref, *rest):
+    outs, pieces = rest[:-1], rest[-1]
+    rows = in_ref.shape[0]
+    chunks = RADIX // pencils // 2
+    offset = offset_ref[0]
+    mine = where_ref[0]
+
+    def step(b, carry):
+        at = pl.ds(pl.multiple_of(b * 8, 8), 8)
+        values = [in_ref[at, n * INNER : (n + 1) * INNER] - offset for n in range(RADIX)]
+        got = real_transform(values)
+        pieces[0, at, :INNER] = got[0][0]
+        pieces[0, at, INNER:] = got[8][0]
+        for s in range(1, 8):
+            pieces[s, at, :INNER] = got[s][0]
+            pieces[s, at, INNER:] = got[s][1]
+        return carry
+
+    lax.fori_loop(0, rows // 8, step, 0)
+    for shift in range(pencils):
+        for chunk in range(chunks):
+            t = lax.rem(mine + shift, pencils) * chunks + chunk
+            total = None
+            for odd in range(2):
+                high, low = split_value(pieces[slot_at(2 * t + odd)])
+                table_high = high_ref[t, 256 * odd : 256 * odd + 256]
+                table_low = low_ref[t, 256 * odd : 256 * odd + 256]
+                part = dot(high, table_high) + dot(low, table_high) + dot(high, table_low)
+                total = part if total is None else total + part
+            for c in range(2):
+                outs[chunk * pencils + shift][c] = total[:, c * 128 : (c + 1) * 128]
+
+
+def shift_columns_kernel(special, pencils, depths, where_ref, *refs):
+    ins, refs = refs[:pencils], refs[pencils:]
+    phase_ref, kern_ref, mirror_ref, edge_ref, turns_ref, late_ref, table_ref = refs[:7]
+    outs, (pieces, waves) = refs[7:-2], refs[-2:]
+    part_rows = ins[0].shape[1]
+    out_rows, lanes = outs[0].shape[1:]
+    share = mirror_ref.shape[1]
+    steps = RADIX // share
+    mine = where_ref[0]
+    now = pl.program_id(0)
+    from_lane = lax.broadcasted_iota(jnp.int32, (kern_ref.shape[2], lanes), 0)
+    to_lane = lax.broadcasted_iota(jnp.int32, (kern_ref.shape[2], lanes), 1)
+    wanted = to_lane + jnp.where(to_lane < HALF, 0, HALF)
+    pick = jnp.where(from_lane == wanted, 0.5, 0.0).astype(bf16)
+    zero_swap = swapped(mine >= 0, (INNER, INNER), 0)
+    plain_swap = swapped(mine < 0, (INNER, INNER), 0)
+
+    def forward(b, carry):
+        values = []
+        for n in range(RADIX):
+            source, begin = divmod(n * INNER, part_rows)
+            at = pl.ds(pl.multiple_of(begin + b * 8, 8), 8)
+            values.append((ins[source][0, at, :], ins[source][1, at, :]))
+        at = pl.ds(pl.multiple_of(b * 8, 8), 8)
+        also = pl.ds(pl.multiple_of(INNER + b * 8, 8), 8)
+        for r, (re, im) in enumerate(transform(values, -1)):
+            pieces[r, at, :] = re
+            pieces[r, also, :] = im
+        return carry
+
+    @pl.when(now == 0)
+    def _():
+        lax.fori_loop(0, INNER // 8, forward, 0)
+
+    def turn(ref, r, u):
+        c, s = ref[u, :, 0:1], ref[u, :, 1:2]
+        pc, ps = phase_ref[r, 0], phase_ref[r, 1]
+        return c * pc - s * ps, s * pc + c * ps
+
+    def wave(r, u):
+        re, im = pieces[r, :INNER], pieces[r, INNER:]
+        c, s = turn(turns_ref, r, u)
+        high, low = split_value(jnp.concatenate([re * c + im * s, im * c - re * s], axis=0))
+        return dot(table_ref[0], high) + dot(table_ref[0], low) + dot(table_ref[1], high)
+
+    def finish(r, u, got):
+        re, im = got[:INNER], got[INNER:]
+        tiles = [mirror_ref[j, u] for j in range(mirror_ref.shape[0])]
+        rows = slice(u * INNER, (u + 1) * INNER)
+        parts = []
+        for c in range(2):
+            other = [tile[:, c * HALF : (c + 1) * HALF] for tile in tiles]
+            other = jnp.concatenate(other, axis=1)
+            own = dot(kern_ref[c, rows, :], pick)
+            parts.append(own + 0.5 * other if c == 0 else own - 0.5 * other)
+        kr, ki = parts
+        if special:
+            other = lax.rem(RADIX - r, RADIX)
+            high, low = split_value(waves[other])
+            swap = jnp.where(r == 0, zero_swap.astype(f32), plain_swap.astype(f32)).astype(bf16) if u == 0 else plain_swap
+            ore = dot(swap, high[:INNER]) + dot(swap, low[:INNER])
+            oim = -(dot(swap, high[INNER:]) + dot(swap, low[INNER:]))
+            mask = (lax.broadcasted_iota(jnp.int32, (INNER, lanes), 1) == 0) & (where_ref[2] == 0)
+            hr = jnp.where(mask, 0.5 * (kr - edge_ref[0, u]), 0.0)
+            hi = jnp.where(mask, 0.5 * (ki - edge_ref[1, u]), 0.0)
+            kr, ki = kr - hr, ki - hi
+            sr = re * kr - im * ki + (ore * hr - oim * hi)
+            si = re * ki + im * kr + (ore * hi + oim * hr)
+        else:
+            sr, si = re * kr - im * ki, re * ki + im * kr
+        spectrum = jnp.concatenate([sr, si], axis=0)
+        high, low = split_value(spectrum)
+        got = dot(table_ref[2], high) + dot(table_ref[2], low) + dot(table_ref[3], high)
+        re, im = got[:INNER], got[INNER:]
+        c, s = turn(late_ref, r, u)
+        pieces[r, :INNER] = re * c - im * s
+        pieces[r, INNER:] = im * c + re * s
+
+    if special:
+        @pl.when(now < steps)
+        def _():
+            for u in range(share):
+                waves[now * share + u] = wave(now * share + u, u)
+
+        @pl.when(now >= steps)
+        def _():
+            for u in range(share):
+                r = (now - steps) * share + u
+                finish(r, u, waves[r])
+    else:
+        for u in range(share):
+            r = now * share + u
+            finish(r, u, wave(r, u))
+
+    def backward(owner, b, carry):
+        at = pl.ds(pl.multiple_of(b * 8, 8), 8)
+        also = pl.ds(pl.multiple_of(INNER + b * 8, 8), 8)
+        values = [(pieces[r, at, :], pieces[r, also, :]) for r in range(RADIX)]
+        for n, (re, im) in enumerate(transform(values, 1)):
+            part, begin = divmod(n * INNER, out_rows)
+            shift, depth = divmod(part, depths)
+            put = pl.ds(pl.multiple_of(begin + b * 8, 8), 8)
+            out_ref = outs[(depth - owner) % depths * pencils + shift]
+            out_ref[0, put, :] = re
+            out_ref[1, put, :] = im
+        return carry
+
+    for owner in range(depths):
+        @pl.when((now == pl.num_programs(0) - 1) & (mine == owner))
+        def _(owner=owner):
+            lax.fori_loop(0, INNER // 8, functools.partial(backward, owner), 0)
+
+
+def shift_fields_kernel(pencils, chunks, where_ref, *refs):
+    ins, at = [], 0
+    for chunk in range(chunks):
+        for shift in range(pencils):
+            count = 2 if shift == 0 else 1
+            ins.append((chunk, shift, refs[at : at + count]))
+            at += count
+    high_ref, low_ref, out_ref, pieces = refs[at:]
+    rows = out_ref.shape[1]
+    mine = where_ref[0]
+    pieces[...] = jnp.zeros_like(pieces)
+    for chunk, shift, found in ins:
+        t = lax.rem(mine + pencils - shift, pencils) * chunks + chunk
+        value = [found[0][c] if len(found) == 1 else found[0][c] + found[1][c] for c in range(2)]
+        high, low = split_value(jnp.concatenate(value, axis=1))
+        for odd in range(2):
+            r = 2 * t + odd
+            slot = slot_at(r)
+            pieces[slot] += dot(high, high_ref[r]) + dot(low, high_ref[r]) + dot(high, low_ref[r])
+
+    def step(b, carry):
+        at = pl.ds(pl.multiple_of(b * 8, 8), 8)
+        values = [(pieces[0, at, :INNER], None)]
+        for s in range(1, 8):
+            values.append((pieces[s, at, :INNER], pieces[s, at, INNER:]))
+        values.append((pieces[0, at, INNER:], None))
+        for n, value in enumerate(real_inverse(values)):
+            out_ref[0, at, n * INNER : (n + 1) * INNER] = value
+        return carry
+
+    lax.fori_loop(0, rows // 8, step, 0)
+
+
 def params(**more):
     return pltpu.CompilerParams(vmem_limit_bytes=48 * 1024 * 1024, **more)
 
 
-def body(density, background, member_ids, layer_kernel, kernel_spectra):
+def wide_body(density, background, member_ids, layer_kernel, kernel_spectra):
     pencils = lax.axis_size("pencil")
     depths = lax.axis_size("depth")
     sharers = lax.axis_size("grp") * lax.axis_size("mem")
@@ -542,6 +725,175 @@
     )(*fields, back_high, back_low)
 
 
+def shift_body(density, background, member_ids, layer_kernel, kernel_spectra):
+    pencils = lax.axis_size("pencil")
+    depths = lax.axis_size("depth")
+    sharers = lax.axis_size("grp") * lax.axis_size("mem")
+    pencil = lax.axis_index("pencil")
+    per = RADIX // pencils
+    chunks = per // 2
+    lanes = 2 * HALF
+    part_rows = density.shape[2]
+    out_rows = part_rows // depths
+    vmem = pl.BlockSpec(memory_space=pltpu.VMEM)
+    smem = pl.BlockSpec(memory_space=pltpu.SMEM)
+
+    def shifted(value, shift):
+        return lax.ppermute(value, "pencil", [(p, (p + shift) % pencils) for p in range(pencils)])
+
+    kern_count = kernel_spectra.shape[0]
+    local = layer_kernel[0] - lax.axis_index("depth") * kern_count
+    share = RADIX // sharers
+    first = lax.axis_index(("grp", "mem")) * share
+    moved = pl.pallas_call(
+        functools.partial(mirror_kernel, share),
+        grid_spec=pltpu.PrefetchScalarGridSpec(
+            num_scalar_prefetch=1,
+            grid=(1,),
+            in_specs=[
+                pl.BlockSpec(
+                    (None, 2, INNER, per * INNER),
+                    lambda i, w, u=u: (w[0], 0, lax.rem(RADIX - w[1] - u, RADIX), 0),
+                )
+                for u in range(share)
+            ],
+            out_specs=[pl.BlockSpec((g, share, INNER, INNER), lambda i, w: (0, 0, 0, 0)) for g in (1, per - 1)],
+        ),
+        out_shape=[jax.ShapeDtypeStruct((g, share, INNER, INNER), f32) for g in (1, per - 1)],
+        compiler_params=params(),
+        cost_estimate=pl.CostEstimate(flops=1 << 20, bytes_accessed=2 << 20, transcendentals=0),
+    )(jnp.stack([local, first, pencil]), *[kernel_spectra] * share)
+    mirrored = lax.ppermute(moved[0], "pencil", [(p, (pencils - p) % pencils) for p in range(pencils)])
+    rest = lax.ppermute(moved[1], "pencil", [(p, pencils - 1 - p) for p in range(pencils)])
+
+    offset = lax.dynamic_index_in_dim(background[:, 0], member_ids[0], 0, keepdims=True)
+    row_high, row_low = halves(row_tables())
+    block = min(part_rows, 128)
+    place = pencil.reshape(1)
+    sent = pl.pallas_call(
+        functools.partial(shift_rows_kernel, pencils),
+        grid=(part_rows // block,),
+        in_specs=[
+            smem,
+            smem,
+            pl.BlockSpec((None, None, block, LENGTH), lambda i: (0, 0, i, 0)),
+            pl.BlockSpec((8, 512, 256), lambda i: (0, 0, 0)),
+            pl.BlockSpec((8, 512, 256), lambda i: (0, 0, 0)),
+        ],
+        out_specs=[pl.BlockSpec((2, block, lanes), lambda i: (0, i, 0))] * (chunks * pencils),
+        out_shape=[jax.ShapeDtypeStruct((2, part_rows, lanes), f32)] * (chunks * pencils),
+        scratch_shapes=[pltpu.VMEM((8, block, 256), f32)],
+        compiler_params=params(),
+        cost_estimate=pl.CostEstimate(flops=6 * part_rows * 2 * LENGTH * 512, bytes_accessed=12 << 20, transcendentals=0),
+    )(offset, place, density, row_high, row_low)
+
+    sign = jnp.array([0.5, -0.5], f32)
+    edge = lax.dynamic_slice(kernel_spectra, (local, 0, 0, HALF), (1, 2, LENGTH, 1))
+    edge = edge.reshape(2, RADIX, INNER).astype(f32)
+    flipped = jnp.concatenate([edge[:, :1], edge[:, :0:-1]], axis=1)[..., ::-1]
+    flipped = jnp.concatenate([jnp.roll(flipped[:, :1], 1, axis=2), flipped[:, 1:]], axis=1)
+    edge = 0.5 * edge + sign.reshape(2, 1, 1) * flipped
+    edge = jnp.where(lax.broadcasted_iota(jnp.int32, (lanes,), 0) == 0, edge[..., None], 0.0)
+
+    arrived = []
+    for k in range(chunks):
+        here = [sent[k * pencils]]
+        for shift in range(1, pencils):
+            value = sent[k * pencils + shift]
+            if k > 0:
+                value, arrived[k - 1][shift] = lax.optimization_barrier((value, arrived[k - 1][shift]))
+            here.append(shifted(value, shift))
+        arrived.append(here)
+
+    mirrored = jnp.concatenate([mirrored, rest], axis=0)
+    mirrored, edge, _ = lax.optimization_barrier((mirrored, edge, sent[0]))
+    mirrored = lax.all_gather(mirrored, ("grp", "mem"), axis=0)
+
+    column, column_turns = column_tables()
+    column_turns = jnp.asarray(column_turns)
+    tables = jnp.stack(halves(column) + halves(column.T))
+    angles = 2 * np.pi * np.arange(pencils)[:, None] * np.arange(RADIX)[None, :] / pencils
+    phases = np.stack([np.cos(angles), np.sin(angles)], axis=-1).round(15)
+    phase = lax.dynamic_index_in_dim(jnp.asarray(phases, f32), pencil, 0, keepdims=False)
+    where = jnp.stack([lax.axis_index("depth"), local, pencil])
+    steps = sharers
+    order = [2, 1, 3, 0] if pencils == 4 else list(range(1, pencils)) + [0]
+    fields = []
+    waiting = None
+    for k in range(chunks):
+        special = k == 0
+
+        def early(i, special=special):
+            return jnp.minimum(i, steps - 1) if special else i
+
+        def late(i, special=special):
+            return jnp.maximum(i - steps, 0) if special else i
+
+        here = [arrived[k][-j % pencils] for j in range(pencils)]
+        if waiting is not None:
+            here, waiting = lax.optimization_barrier((here, waiting))
+            fields.append([waiting[0]] + [shifted(waiting[j], j) for j in range(1, pencils)])
+        edge_block = (2, share, INNER, lanes) if special else (2, 1, 8, lanes)
+        piece = jax.ShapeDtypeStruct((2, out_rows, lanes), f32)
+        out = pl.pallas_call(
+            functools.partial(shift_columns_kernel, special, pencils, depths),
+            grid_spec=pltpu.PrefetchScalarGridSpec(
+                num_scalar_prefetch=1,
+                grid=(2 * steps if special else steps,),
+                in_specs=[pl.BlockSpec((2, part_rows, lanes), lambda i, w: (0, 0, 0))] * pencils
+                + [
+                    smem,
+                    pl.BlockSpec((None, 2, share * INNER, 2 * INNER), lambda i, w, k=k, late=late: (w[1], 0, late(i), k)),
+                    pl.BlockSpec((None, 2, share, INNER, INNER), lambda i, w, k=k, late=late: (late(i), k, 0, 0, 0)),
+                    pl.BlockSpec(
+                        edge_block,
+                        (lambda i, w, late=late: (0, late(i), 0, 0)) if special else (lambda i, w: (0, 0, 0, 0)),
+                    ),
+                    pl.BlockSpec((share, INNER, INNER), lambda i, w, early=early: (early(i), 0, 0)),
+                    pl.BlockSpec((share, INNER, INNER), lambda i, w, late=late: (late(i), 0, 0)),
+                    pl.BlockSpec((4, 256, 256), lambda i, w: (0, 0, 0)),
+                ],
+                out_specs=[pl.BlockSpec((2, out_rows, lanes), lambda i, w: (0, 0, 0))] * (depths * pencils),
+                scratch_shapes=[
+                    pltpu.VMEM((RADIX, 256, lanes), f32),
+                    pltpu.VMEM((RADIX if special else 1, 256, lanes), f32),
+                ],
+            ),
+            out_shape=[piece] * (depths * pencils),
+            compiler_params=params(),
+            cost_estimate=pl.CostEstimate(
+                flops=12 * RADIX * 256 * 256 * lanes, bytes_accessed=16 << 20, transcendentals=0
+            ),
+        )(where, *here, phase, kernel_spectra, mirrored, edge, column_turns, column_turns, tables)
+        keep, give = out[:pencils], out[pencils:]
+        waiting = [None] * pencils
+        for j in order:
+            got = lax.ppermute(give[j], "depth", [(0, 1), (1, 0)])
+            waiting[j] = (keep[j], got) if j == 0 else keep[j] + got
+    fields.append([waiting[0]] + [shifted(waiting[j], j) for j in range(1, pencils)])
+    fields = [ref for chunk in fields for ref in (*chunk[0], *chunk[1:])]
+
+    back_high, back_low = halves(inverse_row_tables().reshape(8, 2, 256, 256)[
+        [0 if r == 8 else min(r, RADIX - r) for r in range(RADIX)], [int(r >= 8) for r in range(RADIX)]
+    ])
+    return pl.pallas_call(
+        functools.partial(shift_fields_kernel, pencils, chunks),
+        in_specs=[smem] + [vmem] * (len(fields) + 2),
+        out_specs=vmem,
+        out_shape=jax.ShapeDtypeStruct((1, out_rows, LENGTH), f32),
+        scratch_shapes=[pltpu.VMEM((8, out_rows, 256), f32)],
+        compiler_params=params(),
+        cost_estimate=pl.CostEstimate(flops=6 * out_rows * 2 * LENGTH * 512, bytes_accessed=8 << 20, transcendentals=0),
+    )(place, *fields, back_high, back_low)
+
+
+def body(density, background, member_ids, layer_kernel, kernel_spectra):
+    pencils, depths = lax.axis_size("pencil"), lax.axis_size("depth")
+    narrow = pencils < RADIX and depths == 2 and density.shape[2] // depths % INNER == 0
+    plan = shift_body if narrow else wide_body
+    return plan(density, background, member_ids, layer_kernel, kernel_spectra)
+
+
 def solution(mesh):
     placed = (
         P(("grp", "mem"), "depth", "pencil", None),

time: 241 us -> 251 us (1.041)
  blocking collectives: 77.6 us -> 0 us
  waiting for transfers between devices: 73 us -> 143 us
  starting transfers between devices: 16.2 us -> 34.5 us
    all_to_all x2 -> x0, blocking collectives: 77.6 us -> none  [the longest x1 51.7 us: body(): lax.all_to_all(part, 'pencil', 0, 0, tiled=True)]
    ppermute x4 -> x22, waiting for transfers between devices: 69.2 us -> 143 us  [the longest x12 82.2 us: shifted(): lax.ppermute(value, 'pencil', [(p, (p + shift) % pencils) for p in range(...]
    ppermute x4 -> x22, starting transfers between devices: 2.32 us -> 34.5 us  [the longest x12 22.1 us: shifted(): lax.ppermute(value, 'pencil', [(p, (p + shift) % pencils) for p in range(...]
    all_to_all x2 -> x0, starting transfers between devices: 13.9 us -> none  [the longest x1 7.48 us: body(): fields.append(lax.all_to_all(before, 'pencil', 0, 0, tiled=True))]
    all_to_all x2 -> x0, waiting for transfers between devices: 3.7 us -> none  [the longest x1 3.7 us: body(): lax.all_to_all(part, 'pencil', 0, 0, tiled=True)]
    unnamed x17 -> x29, local copies, waits for them, and re-layouts: 5.05 us -> 2.46 us
  transfers between devices with their start and end apart: 7 -> 23, of which waited for: 4 -> 14; matrix products, arithmetic and copies ran while one was open for 3% -> 2% of each run, Pallas kernels for 14% -> 4%
where the time goes in v1:
time: 251 us; the launch traced here: 247 us
  waiting for transfers between devices  143 us (57%)
  Pallas kernels  43.4 us (17%)
  starting transfers between devices  34.5 us (14%)
  between operations  14.9 us (6%)
  other arithmetic  6.59 us (3%)
  local copies, waits for them, and re-layouts  4.07 us (2%)
    ppermute x12, waiting for transfers between devices, shifted(): lax.ppermute(value, 'pencil', [(p, (p + shift) % pencils) for p in range(...  82.2 us
    ppermute x1, waiting for transfers between devices, shift_body(): lax.ppermute(moved[1], 'pencil', [(p, pencils - 1 - p) for p in range(pen...  34.4 us
    ppermute x8, waiting for transfers between devices, shift_body(): got = lax.ppermute(give[j], 'depth', [(0, 1), (1, 0)])  26.7 us
    pallas_call x2, Pallas kernels, shift_body(): pl.pallas_call(functools.partial(shift_columns_kernel, special, pencils,...  25.4 us
    ppermute x12, starting transfers between devices, shifted(): lax.ppermute(value, 'pencil', [(p, (p + shift) % pencils) for p in range(...  22.1 us
    pallas_call x1, Pallas kernels, shift_body(): pl.pallas_call(functools.partial(shift_rows_kernel, pencils), grid=(part_...  8.9 us
    ppermute x8, starting transfers between devices, shift_body(): got = lax.ppermute(give[j], 'depth', [(0, 1), (1, 0)])  7.38 us
    pallas_call x1, Pallas kernels, shift_body(): pl.pallas_call(functools.partial(shift_fields_kernel, pencils, chunks), i...  5.57 us
  transfers between devices with their start and end apart: 23, of which 14 were waited for; matrix products, arithmetic and copies ran while one was open for 2% of the time, Pallas kernels for 4%

profile of v1, /device:TPU:18, one launch (start us, length us, event | category | flops | bytes accessed | tf_op | source)
XLA Modules:
  0.0 246.7 jit_solution(12041295253085001176)
XLA Ops:
  7.2 0.1 add_add_fusion.1.where_ref
  7.3 3.5 %shard_map.155 = (f32[1,4,128,128]{3,2,1,0:T(8,128)}, f32[3,4,128,128]{3,2,1,0:T(8,128)S(1)}) custom-call(s32[3]{0:T(128)S(1)} %add_add_fusion.1.where_ref, bf16[2,2,2048,512]{3,2,1,0:T(8,128)(2,1)} %refs_5_.3, bf16[2,2,2048,512]{3,2,1,0:T(8,128)(2,1)} %refs_5_.3, bf16[2,2,2048,512]{3,2,1,0:T(8,128)(2,1)} %refs_5_.3, bf16[2,2,2048,512]{3,2,1,0:T(8,128)(2,1)} %refs_5_.3), custom_call_target="tpu_custom_call" | custom-call | flops 1048576 | bytes 2097152 | tf_op jit(solution)/shard_map/pallas_call | solution.py:748
  10.8 3.6 %collective-permute-start.6 = (f32[1,4,128,128]{3,2,1,0:T(8,128)}, f32[1,4,128,128]{3,2,1,0:T(8,128)}, u32[]{:S(2)}, u32[]{:S(2)}) collective-permute-start(f32[1,4,128,128]{3,2,1,0:T(8,128)} %get-tuple-element.62), channel_id=1, source_target_pairs={{0,0},{4,12},{8,8},{12,4},{1,1},{5,13},{9,9},{13,5},{2,2},{6,14},{... | collective-permute-start | bytes 786440 | tf_op jit(solution)/shard_map/ppermute | solution.py:766
  14.3 1.4 collective-permute-start.7
  15.8 2.0 convert_reduce_fusion
  17.7 0.1 slice.30
  18.5 0.1 slice.26
  18.6 0.1 slice.28
  18.7 0.6 constant_dynamic-slice_fusion
  19.3 0.1 fusion
  19.3 8.9 %shard_map.154 = (f32[2,512,128]{2,1,0:T(8,128)S(1)}, f32[2,512,128]{2,1,0:T(8,128)S(1)}, f32[2,512,128]{2,1,0:T(8,128)S(1)}, f32[2,512,128]{2,1,0:T(8,128)S(1)}...) custom-call(f32[1]{0:T(128)} %bitcast.2.offset_ref, ...), custom_call_target="tpu_custom_call" | custom-call | flops 6442450944 | bytes 12582912 | tf_op jit(solution)/shard_map/pallas_call | solution.py:773
  28.3 0.8 copy-done.7
  29.0 0.8 copy-done.10
  29.8 0.8 copy-done.11
  30.7 1.9 broadcast_select_fusion.refs_7_
  32.6 0.0 collective-permute-done.6
  32.6 34.4 %collective-permute-done.7 = f32[3,4,128,128]{3,2,1,0:T(8,128)} collective-permute-done((f32[3,4,128,128]{3,2,1,0:T(8,128)S(1)}, f32[3,4,128,128]{3,2,1,0:T(8,128)}, u32[]{:S(2)}, u32[]{:S(2)}) %collective-permute-start.7) | collective-permute-done | bytes 786464 | tf_op jit(solution)/shard_map/ppermute | solution.py:767
  67.0 2.3 pad_maximum_fusion
  69.3 0.0 all-gather.3.cloned.1.call-update
  69.3 0.1 collective-permute-start
  69.4 0.1 collective-permute-start.2
  69.4 1.9 collective-permute-start.4
  71.4 0.7 dynamic-slice_bitcast_fusion
  72.1 0.1 copy.21.refs_4_
  72.1 0.1 add_add_fusion.where_ref
  72.2 12.2 %collective-permute-done.refs_1_ = f32[2,512,128]{2,1,0:T(8,128)S(1)} collective-permute-done((f32[2,512,128]{2,1,0:T(8,128)}, f32[2,512,128]{2,1,0:T(8,128)S(1)}, u32[]{:S(2)}, u32[]{:S(2)}) %collective-permute-start) | collective-permute-done | bytes 524320 | tf_op jit(solution)/shard_map/ppermute | solution.py:742
  84.4 29.7 %collective-permute-done.2.refs_2_ = f32[2,512,128]{2,1,0:T(8,128)} collective-permute-done((f32[2,512,128]{2,1,0:T(8,128)}, f32[2,512,128]{2,1,0:T(8,128)}, u32[]{:S(2)}, u32[]{:S(2)}) %collective-permute-start.2) | collective-permute-done | bytes 524320 | tf_op jit(solution)/shard_map/ppermute | solution.py:742
  114.2 0.0 collective-permute-done.4.refs_3_
  114.2 14.1 %shard_map.156 = (f32[2,256,128]{2,1,0:T(8,128)S(1)}, f32[2,256,128]{2,1,0:T(8,128)S(1)}, f32[2,256,128]{2,1,0:T(8,128)S(1)}, f32[2,256,128]{2,1,0:T(8,128)S(1)}...) custom-call(s32[3]{0:T(128)S(1)} %add_add_fusion.where_ref, ...), custom_call_target="tpu_custom_call" | custom-call | flops 1610612736 | bytes 16777216 | tf_op jit(solution)/shard_map/pallas_call | solution.py:838
  128.3 0.6 collective-permute-start.9
  129.0 0.0 collective-permute-start.1
  129.0 3.4 %collective-permute-start.3 = (f32[2,512,128]{2,1,0:T(8,128)S(1)}, f32[2,512,128]{2,1,0:T(8,128)S(1)}, u32[]{:S(2)}, u32[]{:S(2)}) collective-permute-start(f32[2,512,128]{2,1,0:T(8,128)S(1)} %copy-done.6), channel_id=1, source_target_pairs={{0,8},{4,12},{8,0},{12,4},{1,9},{5,13},{9,1},{13,5},{2,10},{6,14},... | collective-permute-start | bytes 1572872 | tf_op jit(solution)/shard_map/ppermute | solution.py:742
  132.4 1.5 collective-permute-start.10
  133.9 2.0 collective-permute-start.5
  135.9 1.4 collective-permute-done.9
  137.3 0.0 collective-permute-start.11
  137.3 5.6 %collective-permute-done.10 = f32[2,256,128]{2,1,0:T(8,128)S(1)} collective-permute-done((f32[2,256,128]{2,1,0:T(8,128)S(1)}, f32[2,256,128]{2,1,0:T(8,128)S(1)}, u32[]{:S(2)}, u32[]{:S(2)}) %collective-permute-start.10) | collective-permute-done | bytes 262176 | tf_op jit(solution)/shard_map/ppermute | solution.py:871
  142.9 0.2 collective-permute-start.8
  143.2 5.3 %collective-permute-done.11 = f32[2,256,128]{2,1,0:T(8,128)S(1)} collective-permute-done((f32[2,256,128]{2,1,0:T(8,128)S(1)}, f32[2,256,128]{2,1,0:T(8,128)S(1)}, u32[]{:S(2)}, u32[]{:S(2)}) %collective-permute-start.11) | collective-permute-done | bytes 262176 | tf_op jit(solution)/shard_map/ppermute | solution.py:871
  148.6 15.2 %collective-permute-done.1.refs_1_ = f32[2,512,128]{2,1,0:T(8,128)S(1)} collective-permute-done((f32[2,512,128]{2,1,0:T(8,128)S(1)}, f32[2,512,128]{2,1,0:T(8,128)S(1)}, u32[]{:S(2)}, u32[]{:S(2)}) %collective-permute-start.1) | collective-permute-done | bytes 524320 | tf_op jit(solution)/shard_map/ppermute | solution.py:742
  163.8 8.7 %collective-permute-done.3.refs_2_ = f32[2,512,128]{2,1,0:T(8,128)S(1)} collective-permute-done((f32[2,512,128]{2,1,0:T(8,128)S(1)}, f32[2,512,128]{2,1,0:T(8,128)S(1)}, u32[]{:S(2)}, u32[]{:S(2)}) %collective-permute-start.3) | collective-permute-done | bytes 524320 | tf_op jit(solution)/shard_map/ppermute | solution.py:742
  172.6 3.9 %collective-permute-done.5.refs_3_ = f32[2,512,128]{2,1,0:T(8,128)S(1)} collective-permute-done((f32[2,512,128]{2,1,0:T(8,128)S(1)}, f32[2,512,128]{2,1,0:T(8,128)S(1)}, u32[]{:S(2)}, u32[]{:S(2)}) %collective-permute-start.5) | collective-permute-done | bytes 524320 | tf_op jit(solution)/shard_map/ppermute | solution.py:742
  176.4 0.0 collective-permute-done.8.refs_1_
  176.4 11.3 %shard_map.157 = (f32[2,256,128]{2,1,0:T(8,128)S(1)}, f32[2,256,128]{2,1,0:T(8,128)S(1)}, f32[2,256,128]{2,1,0:T(8,128)S(1)}, f32[2,256,128]{2,1,0:T(8,128)S(1)}...) custom-call(s32[3]{0:T(128)S(1)} %add_add_fusion.where_ref, ...), custom_call_target="tpu_custom_call" | custom-call | flops 1610612736 | bytes 16777216 | tf_op jit(solution)/shard_map/pallas_call | solution.py:838
  187.7 0.0 copy-start.12
  187.8 1.5 collective-permute-start.16
  189.3 0.5 collective-permute-start.18
  189.8 1.5 collective-permute-start.20
  191.3 0.0 collective-permute-start.12
  191.3 1.0 collective-permute-start.13
  192.3 4.6 %collective-permute-done.16 = f32[2,256,128]{2,1,0:T(8,128)S(1)} collective-permute-done((f32[2,256,128]{2,1,0:T(8,128)S(1)}, f32[2,256,128]{2,1,0:T(8,128)S(1)}, u32[]{:S(2)}, u32[]{:S(2)}) %collective-permute-start.16) | collective-permute-done | bytes 262176 | tf_op jit(solution)/shard_map/ppermute | solution.py:871
  197.0 0.0 collective-permute-start.14
  197.0 5.6 %collective-permute-done.18 = f32[2,256,128]{2,1,0:T(8,128)S(1)} collective-permute-done((f32[2,256,128]{2,1,0:T(8,128)S(1)}, f32[2,256,128]{2,1,0:T(8,128)S(1)}, u32[]{:S(2)}, u32[]{:S(2)}) %collective-permute-start.18) | collective-permute-done | bytes 262176 | tf_op jit(solution)/shard_map/ppermute | solution.py:871
  202.6 1.5 collective-permute-start.15
  204.1 4.1 %collective-permute-done.20 = f32[2,256,128]{2,1,0:T(8,128)S(1)} collective-permute-done((f32[2,256,128]{2,1,0:T(8,128)S(1)}, f32[2,256,128]{2,1,0:T(8,128)S(1)}, u32[]{:S(2)}, u32[]{:S(2)}) %collective-permute-start.20) | collective-permute-done | bytes 262176 | tf_op jit(solution)/shard_map/ppermute | solution.py:871
  208.2 0.0 collective-permute-start.17
  208.3 3.5 %collective-permute-done.12.refs_2_ = f32[2,256,128]{2,1,0:T(8,128)S(1)} collective-permute-done((f32[2,256,128]{2,1,0:T(8,128)S(1)}, f32[2,256,128]{2,1,0:T(8,128)S(1)}, u32[]{:S(2)}, u32[]{:S(2)}) %collective-permute-start.12) | collective-permute-done | bytes 262176 | tf_op jit(solution)/shard_map/ppermute | solution.py:742
  211.8 0.0 collective-permute-start.19
  211.8 0.0 collective-permute-done.13.refs_3_
  211.8 13.6 %collective-permute-start.21 = (f32[2,256,128]{2,1,0:T(8,128)S(1)}, f32[2,256,128]{2,1,0:T(8,128)S(1)}, u32[]{:S(2)}, u32[]{:S(2)}) collective-permute-start(f32[2,256,128]{2,1,0:T(8,128)S(1)} %add.49), channel_id=1, source_target_pairs={{0,12},{4,0},{8,4},{12,8},{1,13},{5,1},{9,5},{13,9},{2,14},{6,2},{... | collective-permute-start | bytes 786440 | tf_op jit(solution)/shard_map/ppermute | solution.py:742
  225.4 8.9 %collective-permute-done.17.refs_7_ = f32[2,256,128]{2,1,0:T(8,128)S(1)} collective-permute-done((f32[2,256,128]{2,1,0:T(8,128)S(1)}, f32[2,256,128]{2,1,0:T(8,128)S(1)}, u32[]{:S(2)}, u32[]{:S(2)}) %collective-permute-start.17) | collective-permute-done | bytes 262176 | tf_op jit(solution)/shard_map/ppermute | solution.py:742
  234.3 0.0 collective-permute-done.19.refs_8_
  234.3 0.0 collective-permute-done.21.refs_9_
  234.3 5.6 %shard_map.158 = f32[1,256,2048]{2,1,0:T(8,128)} custom-call(s32[1]{0:T(128)} %bitcast.where_ref, f32[2,256,128]{2,1,0:T(8,128)S(1)} %get-tuple-element.74.refs_0_, f32[2,256,128]{2,1,0:T(8,128)S(1)} %collective-permute-done.8.refs_1_, f32[2,256,128]{2,1,0:T(8,128)S(1)} %collective-permute-done.12.refs_2_, ...), custom_call_target="tpu_custom_call" | custom-call | flops 3221225472 | bytes 8388608 | tf_op jit(solution)/shard_map/pallas_call | solution.py:879
  (38 shorter events, 0.2 us)
Async XLA Ops:
  6.5 12.1 %copy-start = (f32[8,1]{0,1:T(1,128)S(1)}, f32[8,1]{0,1:T(1,128)}, u32[]{:S(2)}) copy-start(f32[8,1]{0,1:T(1,128)} %param.17) | copy-start | bytes 100
  6.5 107.6 %all-gather.3.cloned.1.call-start = ((), (), s32[]{:S(2)}) async-start(), calls=%async_computation | async-start | bytes 5242880 | tf_op jit(solution)/shard_map/all_gather | solution.py:810
  7.3 12.0 %copy-start.13 = (f32[2]{0:T(128)S(1)}, f32[2]{0:T(128)}, u32[]{:S(2)}) copy-start(f32[2]{0:T(128)} %constant.62.clone) | copy-start | bytes 28
  10.8 21.8 %collective-permute-start.6 = (f32[1,4,128,128]{3,2,1,0:T(8,128)}, f32[1,4,128,128]{3,2,1,0:T(8,128)}, u32[]{:S(2)}, u32[]{:S(2)}) collective-permute-start(f32[1,4,128,128]{3,2,1,0:T(8,128)} %get-tuple-element.62), channel_id=1, source_target_pairs={{0,0},{4,12},{8,8},{12,4},{1,1},{5,13},{9,9},{13,5},{2,2},{6,14},{... | collective-permute-start | bytes 786440 | tf_op jit(solution)/shard_map/ppermute | solution.py:766
  14.3 52.6 %collective-permute-start.7 = (f32[3,4,128,128]{3,2,1,0:T(8,128)S(1)}, f32[3,4,128,128]{3,2,1,0:T(8,128)}, u32[]{:S(2)}, u32[]{:S(2)}) collective-permute-start(f32[3,4,128,128]{3,2,1,0:T(8,128)S(1)} %get-tuple-element.63), channel_id=1, source_target_pairs={{0,12},{4,8},{8,4},{12,0},{1,13},{5,9},{9,5},{13,1},{2,14},{6,10},... | collective-permute-start | bytes 2359304 | tf_op jit(solution)/shard_map/ppermute | solution.py:767
  28.2 0.8 copy-start.7
  29.0 0.8 copy-start.10
  29.8 0.9 copy-start.11
  30.7 36.3 %copy-start.3 = (f32[2,512,128]{2,1,0:T(8,128)}, f32[2,512,128]{2,1,0:T(8,128)S(1)}, u32[]{:S(2)}) copy-start(f32[2,512,128]{2,1,0:T(8,128)S(1)} %get-tuple-element.57) | copy-start | bytes 1572868
  30.7 36.3 %copy-start.5 = (f32[2,512,128]{2,1,0:T(8,128)}, f32[2,512,128]{2,1,0:T(8,128)S(1)}, u32[]{:S(2)}) copy-start(f32[2,512,128]{2,1,0:T(8,128)S(1)} %get-tuple-element.54) | copy-start | bytes 1572868
  30.7 36.3 %copy-start.9 = (f32[2,512,128]{2,1,0:T(8,128)}, f32[2,512,128]{2,1,0:T(8,128)S(1)}, u32[]{:S(2)}) copy-start(f32[2,512,128]{2,1,0:T(8,128)S(1)} %get-tuple-element.56) | copy-start | bytes 1572868
  32.6 81.6 %copy-start.1 = (f32[16,128,128]{2,1,0:T(8,128)S(1)}, f32[16,128,128]{2,1,0:T(8,128)}, u32[]{:S(2)}) copy-start(f32[16,128,128]{2,1,0:T(8,128)} %constant.63.clone.refs_8_.refs_9_) | copy-start | bytes 3145732
  32.6 81.6 %copy-start.2 = (bf16[4,256,256]{2,1,0:T(8,128)(2,1)S(1)}, bf16[4,256,256]{2,1,0:T(8,128)(2,1)}, u32[]{:S(2)}) copy-start(bf16[4,256,256]{2,1,0:T(8,128)(2,1)} %constant.79.refs_10_) | copy-start | bytes 1572868
  69.3 15.1 %collective-permute-start = (f32[2,512,128]{2,1,0:T(8,128)}, f32[2,512,128]{2,1,0:T(8,128)S(1)}, u32[]{:S(2)}, u32[]{:S(2)}) collective-permute-start(f32[2,512,128]{2,1,0:T(8,128)} %copy-done.11), channel_id=1, source_target_pairs={{0,12},{4,0},{8,4},{12,8},{1,13},{5,1},{9,5},{13,9},{2,14},{6,2},{... | collective-permute-start | bytes 1572872 | tf_op jit(solution)/shard_map/ppermute | solution.py:742
  69.4 44.8 %collective-permute-start.2 = (f32[2,512,128]{2,1,0:T(8,128)}, f32[2,512,128]{2,1,0:T(8,128)}, u32[]{:S(2)}, u32[]{:S(2)}) collective-permute-start(f32[2,512,128]{2,1,0:T(8,128)} %copy-done.10), channel_id=1, source_target_pairs={{0,8},{4,12},{8,0},{12,4},{1,9},{5,13},{9,1},{13,5},{2,10},{6,14},... | collective-permute-start | bytes 1572872 | tf_op jit(solution)/shard_map/ppermute | solution.py:742
  69.4 44.7 %collective-permute-start.4 = (f32[2,512,128]{2,1,0:T(8,128)}, f32[2,512,128]{2,1,0:T(8,128)}, u32[]{:S(2)}, u32[]{:S(2)}) collective-permute-start(f32[2,512,128]{2,1,0:T(8,128)} %copy-done.9), channel_id=1, source_target_pairs={{0,4},{4,8},{8,12},{12,0},{1,5},{5,9},{9,13},{13,1},{2,6},{6,10},{... | collective-permute-start | bytes 1572872 | tf_op jit(solution)/shard_map/ppermute | solution.py:742
  114.2 14.8 %copy-start.8 = (f32[2,512,128]{2,1,0:T(8,128)S(1)}, f32[2,512,128]{2,1,0:T(8,128)}, u32[]{:S(2)}) copy-start(f32[2,512,128]{2,1,0:T(8,128)} %copy-done.7) | copy-start | bytes 1572868
  114.2 14.8 %copy-start.6 = (f32[2,512,128]{2,1,0:T(8,128)S(1)}, f32[2,512,128]{2,1,0:T(8,128)}, u32[]{:S(2)}) copy-start(f32[2,512,128]{2,1,0:T(8,128)} %copy-done.5) | copy-start | bytes 1572868
  114.2 19.7 %copy-start.4 = (f32[2,512,128]{2,1,0:T(8,128)S(1)}, f32[2,512,128]{2,1,0:T(8,128)}, u32[]{:S(2)}) copy-start(f32[2,512,128]{2,1,0:T(8,128)} %copy-done.3) | copy-start | bytes 1572868
  128.3 9.0 %collective-permute-start.9 = (f32[2,256,128]{2,1,0:T(8,128)S(1)}, f32[2,256,128]{2,1,0:T(8,128)S(1)}, u32[]{:S(2)}, u32[]{:S(2)}) collective-permute-start(f32[2,256,128]{2,1,0:T(8,128)S(1)} %get-tuple-element.69), channel_id=1, source_target_pairs={{0,2},{2,0},{1,3},{3,1},{4,6},{6,4},{5,7},{7,5},{8,10},{10,8},{9,1... | collective-permute-start | bytes 786440 | tf_op jit(solution)/shard_map/ppermute | solution.py:871
  129.0 34.9 %collective-permute-start.1 = (f32[2,512,128]{2,1,0:T(8,128)S(1)}, f32[2,512,128]{2,1,0:T(8,128)S(1)}, u32[]{:S(2)}, u32[]{:S(2)}) collective-permute-start(f32[2,512,128]{2,1,0:T(8,128)S(1)} %copy-done.8), channel_id=1, source_target_pairs={{0,12},{4,0},{8,4},{12,8},{1,13},{5,1},{9,5},{13,9},{2,14},{6,2},{... | collective-permute-start | bytes 1572872 | tf_op jit(solution)/shard_map/ppermute | solution.py:742
  129.0 43.6 %collective-permute-start.3 = (f32[2,512,128]{2,1,0:T(8,128)S(1)}, f32[2,512,128]{2,1,0:T(8,128)S(1)}, u32[]{:S(2)}, u32[]{:S(2)}) collective-permute-start(f32[2,512,128]{2,1,0:T(8,128)S(1)} %copy-done.6), channel_id=1, source_target_pairs={{0,8},{4,12},{8,0},{12,4},{1,9},{5,13},{9,1},{13,5},{2,10},{6,14},... | collective-permute-start | bytes 1572872 | tf_op jit(solution)/shard_map/ppermute | solution.py:742
  132.4 10.5 %collective-permute-start.10 = (f32[2,256,128]{2,1,0:T(8,128)S(1)}, f32[2,256,128]{2,1,0:T(8,128)S(1)}, u32[]{:S(2)}, u32[]{:S(2)}) collective-permute-start(f32[2,256,128]{2,1,0:T(8,128)S(1)} %get-tuple-element.71), channel_id=1, source_target_pairs={{0,2},{2,0},{1,3},{3,1},{4,6},{6,4},{5,7},{7,5},{8,10},{10,8},{9,1... | collective-permute-start | bytes 786440 | tf_op jit(solution)/shard_map/ppermute | solution.py:871
  133.9 42.5 %collective-permute-start.5 = (f32[2,512,128]{2,1,0:T(8,128)S(1)}, f32[2,512,128]{2,1,0:T(8,128)S(1)}, u32[]{:S(2)}, u32[]{:S(2)}) collective-permute-start(f32[2,512,128]{2,1,0:T(8,128)S(1)} %copy-done.4), channel_id=1, source_target_pairs={{0,4},{4,8},{8,12},{12,0},{1,5},{5,9},{9,13},{13,1},{2,6},{6,10},{... | collective-permute-start | bytes 1572872 | tf_op jit(solution)/shard_map/ppermute | solution.py:742
  137.3 11.2 %collective-permute-start.11 = (f32[2,256,128]{2,1,0:T(8,128)S(1)}, f32[2,256,128]{2,1,0:T(8,128)S(1)}, u32[]{:S(2)}, u32[]{:S(2)}) collective-permute-start(f32[2,256,128]{2,1,0:T(8,128)S(1)} %get-tuple-element.73), channel_id=1, source_target_pairs={{0,2},{2,0},{1,3},{3,1},{4,6},{6,4},{5,7},{7,5},{8,10},{10,8},{9,1... | collective-permute-start | bytes 786440 | tf_op jit(solution)/shard_map/ppermute | solution.py:871
  142.9 33.5 %collective-permute-start.8 = (f32[2,256,128]{2,1,0:T(8,128)S(1)}, f32[2,256,128]{2,1,0:T(8,128)S(1)}, u32[]{:S(2)}, u32[]{:S(2)}) collective-permute-start(f32[2,256,128]{2,1,0:T(8,128)S(1)} %get-tuple-element.67), channel_id=1, source_target_pairs={{0,2},{2,0},{1,3},{3,1},{4,6},{6,4},{5,7},{7,5},{8,10},{10,8},{9,1... | collective-permute-start | bytes 786440 | tf_op jit(solution)/shard_map/ppermute | solution.py:871
  187.7 46.5 %copy-start.12 = (bf16[16,256,256]{2,1,0:T(8,128)(2,1)S(1)}, bf16[16,256,256]{2,1,0:T(8,128)(2,1)}, u32[]{:S(2)}) copy-start(bf16[16,256,256]{2,1,0:T(8,128)(2,1)} %constant.69.clone.refs_10_) | copy-start | bytes 6291460
  187.8 9.2 %collective-permute-start.16 = (f32[2,256,128]{2,1,0:T(8,128)S(1)}, f32[2,256,128]{2,1,0:T(8,128)S(1)}, u32[]{:S(2)}, u32[]{:S(2)}) collective-permute-start(f32[2,256,128]{2,1,0:T(8,128)S(1)} %get-tuple-element.86), channel_id=1, source_target_pairs={{0,2},{2,0},{1,3},{3,1},{4,6},{6,4},{5,7},{7,5},{8,10},{10,8},{9,1... | collective-permute-start | bytes 786440 | tf_op jit(solution)/shard_map/ppermute | solution.py:871
  189.3 13.3 %collective-permute-start.18 = (f32[2,256,128]{2,1,0:T(8,128)S(1)}, f32[2,256,128]{2,1,0:T(8,128)S(1)}, u32[]{:S(2)}, u32[]{:S(2)}) collective-permute-start(f32[2,256,128]{2,1,0:T(8,128)S(1)} %get-tuple-element.88), channel_id=1, source_target_pairs={{0,2},{2,0},{1,3},{3,1},{4,6},{6,4},{5,7},{7,5},{8,10},{10,8},{9,1... | collective-permute-start | bytes 786440 | tf_op jit(solution)/shard_map/ppermute | solution.py:871
  189.8 18.4 %collective-permute-start.20 = (f32[2,256,128]{2,1,0:T(8,128)S(1)}, f32[2,256,128]{2,1,0:T(8,128)S(1)}, u32[]{:S(2)}, u32[]{:S(2)}) collective-permute-start(f32[2,256,128]{2,1,0:T(8,128)S(1)} %get-tuple-element.90), channel_id=1, source_target_pairs={{0,2},{2,0},{1,3},{3,1},{4,6},{6,4},{5,7},{7,5},{8,10},{10,8},{9,1... | collective-permute-start | bytes 786440 | tf_op jit(solution)/shard_map/ppermute | solution.py:871
  191.3 20.5 %collective-permute-start.12 = (f32[2,256,128]{2,1,0:T(8,128)S(1)}, f32[2,256,128]{2,1,0:T(8,128)S(1)}, u32[]{:S(2)}, u32[]{:S(2)}) collective-permute-start(f32[2,256,128]{2,1,0:T(8,128)S(1)} %add.44), channel_id=1, source_target_pairs={{0,4},{4,8},{8,12},{12,0},{1,5},{5,9},{9,13},{13,1},{2,6},{6,10},{... | collective-permute-start | bytes 786440 | tf_op jit(solution)/shard_map/ppermute | solution.py:742
  191.3 20.5 %collective-permute-start.13 = (f32[2,256,128]{2,1,0:T(8,128)S(1)}, f32[2,256,128]{2,1,0:T(8,128)S(1)}, u32[]{:S(2)}, u32[]{:S(2)}) collective-permute-start(f32[2,256,128]{2,1,0:T(8,128)S(1)} %add.45), channel_id=1, source_target_pairs={{0,8},{4,12},{8,0},{12,4},{1,9},{5,13},{9,1},{13,5},{2,10},{6,14},... | collective-permute-start | bytes 786440 | tf_op jit(solution)/shard_map/ppermute | solution.py:742
  197.0 28.4 %collective-permute-start.14 = (f32[2,256,128]{2,1,0:T(8,128)S(1)}, f32[2,256,128]{2,1,0:T(8,128)S(1)}, u32[]{:S(2)}, u32[]{:S(2)}) collective-permute-start(f32[2,256,128]{2,1,0:T(8,128)S(1)} %add.46), channel_id=1, source_target_pairs={{0,12},{4,0},{8,4},{12,8},{1,13},{5,1},{9,5},{13,9},{2,14},{6,2},{... | collective-permute-start | bytes 786440 | tf_op jit(solution)/shard_map/ppermute | solution.py:742
  202.6 22.8 %collective-permute-start.15 = (f32[2,256,128]{2,1,0:T(8,128)S(1)}, f32[2,256,128]{2,1,0:T(8,128)S(1)}, u32[]{:S(2)}, u32[]{:S(2)}) collective-permute-start(f32[2,256,128]{2,1,0:T(8,128)S(1)} %get-tuple-element.84), channel_id=1, source_target_pairs={{0,2},{2,0},{1,3},{3,1},{4,6},{6,4},{5,7},{7,5},{8,10},{10,8},{9,1... | collective-permute-start | bytes 786440 | tf_op jit(solution)/shard_map/ppermute | solution.py:871
  208.2 26.1 %collective-permute-start.17 = (f32[2,256,128]{2,1,0:T(8,128)S(1)}, f32[2,256,128]{2,1,0:T(8,128)S(1)}, u32[]{:S(2)}, u32[]{:S(2)}) collective-permute-start(f32[2,256,128]{2,1,0:T(8,128)S(1)} %add.47), channel_id=1, source_target_pairs={{0,4},{4,8},{8,12},{12,0},{1,5},{5,9},{9,13},{13,1},{2,6},{6,10},{... | collective-permute-start | bytes 786440 | tf_op jit(solution)/shard_map/ppermute | solution.py:742
  211.8 22.5 %collective-permute-start.19 = (f32[2,256,128]{2,1,0:T(8,128)S(1)}, f32[2,256,128]{2,1,0:T(8,128)S(1)}, u32[]{:S(2)}, u32[]{:S(2)}) collective-permute-start(f32[2,256,128]{2,1,0:T(8,128)S(1)} %add.48), channel_id=1, source_target_pairs={{0,8},{4,12},{8,0},{12,4},{1,9},{5,13},{9,1},{13,5},{2,10},{6,14},... | collective-permute-start | bytes 786440 | tf_op jit(solution)/shard_map/ppermute | solution.py:742
  211.8 22.5 %collective-permute-start.21 = (f32[2,256,128]{2,1,0:T(8,128)S(1)}, f32[2,256,128]{2,1,0:T(8,128)S(1)}, u32[]{:S(2)}, u32[]{:S(2)}) collective-permute-start(f32[2,256,128]{2,1,0:T(8,128)S(1)} %add.49), channel_id=1, source_target_pairs={{0,12},{4,0},{8,4},{12,8},{1,13},{5,1},{9,5},{13,9},{2,14},{6,2},{... | collective-permute-start | bytes 786440 | tf_op jit(solution)/shard_map/ppermute | solution.py:742
Sparse Core Ops, SparseCore 0:
  69.4 34.5 all-gather.2

commit v2 on v0

--- a/solution.py
+++ b/solution.py
@@ -390,11 +390,363 @@
     lax.fori_loop(0, rows // 8, step, 0)
 
 
+def slot_at(r):
+    return jnp.where(r == 8, 0, jnp.minimum(r, RADIX - r))
+
+
+BLOCKS = 4
+
+
+def fused_kernel(pencils, depths, offset_ref, local_ref, phase_ref, density_ref, kern_ref, row_high_ref, row_low_ref,
+                 back_high_ref, back_low_ref, table_ref, turns_ref, out_ref,
+                 dens, source, kern, row_high, row_low, back_high, back_low, tables, turns,
+                 pieces, sending, landing, moved, gathered, spectra, waves, keep, other_keep, fields,
+                 local_sem, b_sem, g_sem, a_send_sem, a_recv_sem, x_sem, c_sem):
+    per = RADIX // pencils
+    chunks = per // 2
+    lanes = 2 * HALF
+    part_rows = dens.shape[0]
+    block = part_rows // BLOCKS
+    out_rows = part_rows // depths
+    share = moved.shape[1]
+    me = lax.axis_index("pencil")
+    deep = lax.axis_index("depth")
+    grp, mem = lax.axis_index("grp"), lax.axis_index("mem")
+    sharer = grp * 2 + mem
+    first = sharer * share
+    local = local_ref[0]
+
+    def remote(src, dst, send, recv, **where):
+        return pltpu.make_async_remote_copy(
+            src_ref=src, dst_ref=dst, send_sem=send, recv_sem=recv,
+            device_id=where, device_id_type=pl.DeviceIdType.MESH,
+        )
+
+    def toward(shift):
+        return lax.rem(me + shift, pencils)
+
+    loads = []
+
+    def load(src, dst):
+        copy = pltpu.make_async_copy(src, dst, local_sem.at[len(loads)])
+        copy.start()
+        loads.append(copy)
+        return copy
+
+    source_loads = [
+        load(kern_ref.at[:, :, pl.ds(pl.multiple_of(lax.rem(RADIX - first - u, RADIX) * INNER, INNER), INNER)], source.at[u])
+        for u in range(share)
+    ]
+    dens_loads = [load(density_ref.at[0, 0, pl.ds(i * block, block)], dens.at[pl.ds(i * block, block)]) for i in range(BLOCKS)]
+    row_loads = [load(row_high_ref, row_high), load(row_low_ref, row_low)]
+    late_loads = [load(table_ref, tables), load(turns_ref, turns), load(kern_ref, kern),
+                  load(back_high_ref, back_high), load(back_low_ref, back_low)]
+
+    barrier = pltpu.get_barrier_semaphore()
+    peers = [{"pencil": toward(shift)} for shift in range(1, pencils)]
+    peers += [{"depth": 1 - deep}, {"grp": 1 - grp}, {"mem": 1 - mem}]
+    for peer in peers:
+        pl.semaphore_signal(barrier, inc=1, device_id=peer, device_id_type=pl.DeviceIdType.MESH)
+
+    for copy in source_loads:
+        copy.wait()
+    plain = swapped(me < 0, (INNER, HALF), 1)
+    edge = swapped(me == 0, (INNER, HALF), 1)
+    for u in range(share):
+        swap = swapped(first + u == 0, (INNER, INNER), 0)
+        rows = [dot(swap, source[u, local, c]).astype(bf16) for c in range(2)]
+        for j in range(per):
+            turn = edge if j == 0 else plain
+            turned = [dot(rows[c][:, j * INNER : (j + 1) * INNER], turn) for c in range(2)]
+            moved[(per - j) % per, u] = jnp.concatenate(turned, axis=1)
+
+    pl.semaphore_wait(barrier, len(peers))
+    rest = remote(moved.at[pl.ds(1, per - 1)], gathered.at[sharer, pl.ds(1, per - 1)], b_sem.at[0], b_sem.at[1],
+                  pencil=pencils - 1 - me)
+    rest.start()
+    partner = lax.rem(pencils - me, pencils)
+    zero = remote(moved.at[0], gathered.at[sharer, 0], b_sem.at[2], b_sem.at[3], pencil=partner)
+    stay = pltpu.make_async_copy(moved.at[0], gathered.at[sharer, 0], b_sem.at[4])
+
+    @pl.when(partner != me)
+    def _():
+        zero.start()
+
+    @pl.when(partner == me)
+    def _():
+        stay.start()
+
+    for copy in row_loads:
+        copy.wait()
+    offset = offset_ref[0]
+
+    def a_copy(chunk, shift, i):
+        at = pl.ds(i * block, block)
+        return remote(sending.at[chunk, shift, :, at], landing.at[chunk, shift - 1, :, at],
+                      a_send_sem.at[chunk, shift - 1, i], a_recv_sem.at[chunk, shift - 1, i], pencil=toward(shift))
+
+    for i in range(BLOCKS):
+        dens_loads[i].wait()
+
+        def step(b, carry, i=i):
+            at = pl.ds(pl.multiple_of(b * 8, 8), 8)
+            here = pl.ds(pl.multiple_of(i * block + b * 8, 8), 8)
+            got = real_transform([dens[here, n * INNER : (n + 1) * INNER] - offset for n in range(RADIX)])
+            pieces[0, at, :INNER] = got[0][0]
+            pieces[0, at, INNER:] = got[8][0]
+            for s in range(1, 8):
+                pieces[s, at, :INNER] = got[s][0]
+                pieces[s, at, INNER:] = got[s][1]
+            return carry
+
+        lax.fori_loop(0, block // 8, step, 0)
+
+        def part(index, carry, i=i):
+            shift, chunk = index // chunks, lax.rem(index, chunks)
+            t = lax.rem(me + shift, pencils) * chunks + chunk
+            total = None
+            for odd in range(2):
+                high, low = split_value(pieces[slot_at(2 * t + odd)])
+                table_high = row_high[t, 256 * odd : 256 * odd + 256]
+                table_low = row_low[t, 256 * odd : 256 * odd + 256]
+                term = dot(high, table_high) + dot(low, table_high) + dot(high, table_low)
+                total = term if total is None else total + term
+            for c in range(2):
+                sending[chunk, shift, c, i * block : (i + 1) * block] = total[:, c * 128 : (c + 1) * 128]
+            return carry
+
+        lax.fori_loop(0, pencils * chunks, part, 0)
+        for shift in SHIFTS:
+            a_copy(0, shift, i).start()
+
+    def start_a(chunk):
+        for shift in SHIFTS:
+            for i in range(BLOCKS):
+                a_copy(chunk, shift, i).start()
+
+    def wait_a(chunk):
+        for shift in SHIFTS:
+            for i in range(BLOCKS):
+                a_copy(chunk, shift, i).wait_recv()
+
+    for copy in late_loads:
+        copy.wait()
+
+    rest.wait_recv()
+
+    @pl.when(partner != me)
+    def _():
+        zero.wait_recv()
+        zero.wait_send()
+
+    @pl.when(partner == me)
+    def _():
+        stay.wait()
+
+    own = gathered.at[sharer]
+    far = (1 - grp) * 2 + mem
+    across = remote(own, own, g_sem.at[0], g_sem.at[1], grp=1 - grp)
+    across.start()
+    beside = remote(own, own, g_sem.at[2], g_sem.at[3], mem=1 - mem)
+    beside.start()
+    if not PACED:
+        start_a(1)
+    across.wait_recv()
+    passed = remote(gathered.at[far], gathered.at[far], g_sem.at[4], g_sem.at[5], mem=1 - mem)
+    passed.start()
+    beside.wait_recv()
+    passed.wait_recv()
+
+    from_lane = lax.broadcasted_iota(jnp.int32, (2 * INNER, lanes), 0)
+    to_lane = lax.broadcasted_iota(jnp.int32, (2 * INNER, lanes), 1)
+    pick = jnp.where(from_lane == to_lane + jnp.where(to_lane < HALF, 0, HALF), 0.5, 0.0).astype(bf16)
+    from_lane, to_lane = from_lane[:INNER], to_lane[:INNER]
+    pick_edge = jnp.where((from_lane == HALF) & (to_lane == 0), 0.5, 0.0).astype(bf16)
+    mask = (to_lane == 0) & (me == 0)
+
+    def turned(r):
+        c, s = turns[r, :, 0:1], turns[r, :, 1:2]
+        pc, ps = phase_ref[me, r, 0], phase_ref[me, r, 1]
+        return c * pc - s * ps, s * pc + c * ps
+
+    def wave(r):
+        re, im = spectra[r, :INNER], spectra[r, INNER:]
+        c, s = turned(r)
+        high, low = split_value(jnp.concatenate([re * c + im * s, im * c - re * s], axis=0))
+        return dot(tables[0], high) + dot(tables[0], low) + dot(tables[1], high)
+
+    def finish(chunk, r, got):
+        re, im = got[:INNER], got[INNER:]
+        rows = pl.ds(pl.multiple_of(r * INNER, INNER), INNER)
+        holder, u = r // share, lax.rem(r, share)
+        parts = []
+        for c in range(2):
+            other = [gathered[holder, 2 * chunk + j, u, :, c * HALF : (c + 1) * HALF] for j in range(2)]
+            other = jnp.concatenate(other, axis=1)
+            mine = dot(kern[local, c, rows, 2 * chunk * INNER : 2 * (chunk + 1) * INNER], pick)
+            parts.append(mine + 0.5 * other if c == 0 else mine - 0.5 * other)
+        kr, ki = parts
+        if chunk == 0:
+            other = lax.rem(RADIX - r, RADIX)
+            other_rows = pl.ds(pl.multiple_of(other * INNER, INNER), INNER)
+            swap = swapped(r == 0, (INNER, INNER), 0)
+            edges = []
+            for c in range(2):
+                mine = dot(kern[local, c, rows, :INNER], pick_edge)
+                flipped = dot(swap, kern[local, c, other_rows, :INNER]).astype(bf16)
+                flipped = dot(flipped, pick_edge)
+                edges.append(mine + flipped if c == 0 else mine - flipped)
+            high, low = split_value(waves[other])
+            ore = dot(swap, high[:INNER]) + dot(swap, low[:INNER])
+            oim = -(dot(swap, high[INNER:]) + dot(swap, low[INNER:]))
+            hr = jnp.where(mask, 0.5 * (kr - edges[0]), 0.0)
+            hi = jnp.where(mask, 0.5 * (ki - edges[1]), 0.0)
+            kr, ki = kr - hr, ki - hi
+            sr = re * kr - im * ki + (ore * hr - oim * hi)
+            si = re * ki + im * kr + (ore * hi + oim * hr)
+        else:
+            sr, si = re * kr - im * ki, re * ki + im * kr
+        high, low = split_value(jnp.concatenate([sr, si], axis=0))
+        got = dot(tables[2], high) + dot(tables[2], low) + dot(tables[3], high)
+        re, im = got[:INNER], got[INNER:]
+        c, s = turned(r)
+        spectra[r, :INNER] = re * c - im * s
+        spectra[r, INNER:] = im * c + re * s
+
+    def columns(chunk):
+        def forward(b, carry):
+            values = []
+            for n in range(RADIX):
+                j, begin = divmod(n * INNER, part_rows)
+                at = pl.ds(pl.multiple_of(begin + b * 8, 8), 8)
+                ref = sending.at[chunk, 0] if j == 0 else landing.at[chunk, pencils - j - 1]
+                values.append((ref[0, at, :], ref[1, at, :]))
+            at = pl.ds(pl.multiple_of(b * 8, 8), 8)
+            also = pl.ds(pl.multiple_of(INNER + b * 8, 8), 8)
+            for r, (re, im) in enumerate(transform(values, -1)):
+                spectra[r, at, :] = re
+                spectra[r, also, :] = im
+            return carry
+
+        lax.fori_loop(0, INNER // 8, forward, 0)
+
+        def early(i, carry):
+            for u in range(UNROLL):
+                waves[i * UNROLL + u] = wave(i * UNROLL + u)
+            return carry
+
+        def late(i, carry):
+            for u in range(UNROLL):
+                r = i * UNROLL + u
+                finish(chunk, r, waves[r] if chunk == 0 else wave(r))
+            return carry
+
+        if chunk == 0:
+            lax.fori_loop(0, RADIX // UNROLL, early, 0)
+        lax.fori_loop(0, RADIX // UNROLL, late, 0)
+
+        def backward(b, carry):
+            at = pl.ds(pl.multiple_of(b * 8, 8), 8)
+            also = pl.ds(pl.multiple_of(INNER + b * 8, 8), 8)
+            values = [(spectra[r, at, :], spectra[r, also, :]) for r in range(RADIX)]
+            for n, (re, im) in enumerate(transform(values, 1)):
+                shift_depth, begin = divmod(n * INNER, out_rows)
+                shift, depth = divmod(shift_depth, depths)
+                put = pl.ds(pl.multiple_of(begin + b * 8, 8), 8)
+                slot = jnp.where(deep == depth, 0, 1)
+                keep[chunk, slot, shift, 0, put, :] = re
+                keep[chunk, slot, shift, 1, put, :] = im
+            return carry
+
+        lax.fori_loop(0, INNER // 8, backward, 0)
+
+    def x_copy(chunk, j):
+        return remote(keep.at[chunk, 1, j], other_keep.at[chunk, j], x_sem.at[0, chunk, j], x_sem.at[1, chunk, j],
+                      depth=1 - deep)
+
+    def c_copy(chunk, j):
+        return remote(keep.at[chunk, 0, j], fields.at[chunk, j - 1], c_sem.at[0, chunk, j - 1], c_sem.at[1, chunk, j - 1],
+                      pencil=toward(j))
+
+    def summed(chunk, j):
+        x_copy(chunk, j).wait_recv()
+        keep[chunk, 0, j] += other_keep[chunk, j]
+
+    def gather_field(chunk, shift):
+        t = lax.rem(me + pencils - shift, pencils) * chunks + chunk
+        ref = keep.at[chunk, 0, 0] if shift == 0 else fields.at[chunk, shift - 1]
+        high, low = split_value(jnp.concatenate([ref[0], ref[1]], axis=1))
+        for odd in range(2):
+            r = 2 * t + odd
+            out_ref[slot_at(r)] += dot(high, back_high[r]) + dot(low, back_high[r]) + dot(high, back_low[r])
+
+    out_ref[...] = jnp.zeros_like(out_ref)
+    wait_a(0)
+    if PACED:
+        start_a(1)
+    columns(0)
+    for j in ORDER:
+        x_copy(0, j).start()
+    for j in ORDER:
+        summed(0, j)
+    wait_a(1)
+    for j in ORDER:
+        if j:
+            c_copy(0, j).start()
+    columns(1)
+    for j in ORDER:
+        x_copy(1, j).start()
+    gather_field(0, 0)
+    for j in ORDER:
+        summed(1, j)
+        if j:
+            c_copy(1, j).start()
+    gather_field(1, 0)
+    for chunk in range(chunks):
+        for j in ORDER:
+            if j:
+                c_copy(chunk, j).wait_recv()
+                gather_field(chunk, j)
+
+    rest.wait_send()
+    across.wait_send()
+    beside.wait_send()
+    passed.wait_send()
+    for chunk in range(chunks):
+        for shift in SHIFTS:
+            for i in range(BLOCKS):
+                a_copy(chunk, shift, i).wait_send()
+        for j in ORDER:
+            x_copy(chunk, j).wait_send()
+            if j:
+                c_copy(chunk, j).wait_send()
+
+
+def last_kernel(pieces, out_ref):
+    def step(b, carry):
+        at = pl.ds(pl.multiple_of(b * 8, 8), 8)
+        values = [(pieces[0, at, :INNER], None)]
+        for s in range(1, 8):
+            values.append((pieces[s, at, :INNER], pieces[s, at, INNER:]))
+        values.append((pieces[0, at, INNER:], None))
+        for n, value in enumerate(real_inverse(values)):
+            out_ref[0, at, n * INNER : (n + 1) * INNER] = value
+        return carry
+
+    lax.fori_loop(0, out_ref.shape[1] // 8, step, 0)
+
+
+SHIFTS = (2, 1, 3)
+ORDER = (2, 1, 3, 0)
+UNROLL = 4
+PACED = True
+
+
 def params(**more):
     return pltpu.CompilerParams(vmem_limit_bytes=48 * 1024 * 1024, **more)
 
 
-def body(density, background, member_ids, layer_kernel, kernel_spectra):
+def wide_body(density, background, member_ids, layer_kernel, kernel_spectra):
     pencils = lax.axis_size("pencil")
     depths = lax.axis_size("depth")
     sharers = lax.axis_size("grp") * lax.axis_size("mem")
@@ -542,6 +894,83 @@
     )(*fields, back_high, back_low)
 
 
+def fused_body(density, background, member_ids, layer_kernel, kernel_spectra):
+    pencils = lax.axis_size("pencil")
+    depths = lax.axis_size("depth")
+    sharers = lax.axis_size("grp") * lax.axis_size("mem")
+    per = RADIX // pencils
+    chunks = per // 2
+    lanes = 2 * HALF
+    part_rows = density.shape[2]
+    out_rows = part_rows // depths
+    share = RADIX // sharers
+    smem = pl.BlockSpec(memory_space=pltpu.SMEM)
+    anywhere = pl.BlockSpec(memory_space=pl.ANY)
+    vmem = pl.BlockSpec(memory_space=pltpu.VMEM)
+
+    offset = lax.dynamic_index_in_dim(background[:, 0], member_ids[0], 0, keepdims=True)
+    local = layer_kernel - lax.axis_index("depth") * kernel_spectra.shape[0]
+    angles = 2 * np.pi * np.arange(pencils)[:, None] * np.arange(RADIX)[None, :] / pencils
+    phases = jnp.asarray(np.stack([np.cos(angles), np.sin(angles)], axis=-1).round(15), f32)
+    row_high, row_low = halves(row_tables())
+    where = [0 if r == 8 else min(r, RADIX - r) for r in range(RADIX)], [int(r >= 8) for r in range(RADIX)]
+    back_high, back_low = halves(inverse_row_tables().reshape(8, 2, 256, 256)[where])
+    column, turns = column_tables()
+    tables = jnp.stack(halves(column) + halves(column.T))
+    turns = jnp.asarray(turns)
+    dma = pltpu.SemaphoreType.DMA
+    pieces = pl.pallas_call(
+        functools.partial(fused_kernel, pencils, depths),
+        in_specs=[smem] * 3 + [anywhere] * 8,
+        out_specs=vmem,
+        out_shape=jax.ShapeDtypeStruct((8, out_rows, 256), f32),
+        scratch_shapes=[
+            pltpu.VMEM((part_rows, LENGTH), f32),
+            pltpu.VMEM((share, kernel_spectra.shape[0], 2, INNER, per * INNER), bf16),
+            pltpu.VMEM(kernel_spectra.shape, bf16),
+            pltpu.VMEM(row_high.shape, bf16),
+            pltpu.VMEM(row_low.shape, bf16),
+            pltpu.VMEM(back_high.shape, bf16),
+            pltpu.VMEM(back_low.shape, bf16),
+            pltpu.VMEM(tables.shape, bf16),
+            pltpu.VMEM(turns.shape, f32),
+            pltpu.VMEM((8, part_rows // BLOCKS, 256), f32),
+            pltpu.VMEM((chunks, pencils, 2, part_rows, lanes), f32),
+            pltpu.VMEM((chunks, pencils - 1, 2, part_rows, lanes), f32),
+            pltpu.VMEM((per, share, INNER, INNER), f32),
+            pltpu.VMEM((sharers, per, share, INNER, INNER), f32),
+            pltpu.VMEM((RADIX, 256, lanes), f32),
+            pltpu.VMEM((RADIX, 256, lanes), f32),
+            pltpu.VMEM((chunks, 2, pencils, 2, out_rows, lanes), f32),
+            pltpu.VMEM((chunks, pencils, 2, out_rows, lanes), f32),
+            pltpu.VMEM((chunks, pencils - 1, 2, out_rows, lanes), f32),
+            dma((share + BLOCKS + 7,)),
+            dma((5,)),
+            dma((6,)),
+            dma((chunks, pencils - 1, BLOCKS)),
+            dma((chunks, pencils - 1, BLOCKS)),
+            dma((2, chunks, pencils)),
+            dma((2, chunks, pencils - 1)),
+        ],
+        compiler_params=pltpu.CompilerParams(
+            vmem_limit_bytes=60 * 1024 * 1024, collective_id=0, has_side_effects=True
+        ),
+    )(offset, local, phases, density, kernel_spectra, row_high, row_low, back_high, back_low, tables, turns)
+    return pl.pallas_call(
+        last_kernel,
+        in_specs=[vmem],
+        out_specs=vmem,
+        out_shape=jax.ShapeDtypeStruct((1, out_rows, LENGTH), f32),
+        compiler_params=params(),
+    )(pieces)
+
+
+def body(density, background, member_ids, layer_kernel, kernel_spectra):
+    sizes = tuple(lax.axis_size(name) for name in ("grp", "pencil", "depth", "mem"))
+    plan = fused_body if sizes == (2, 4, 2, 2) else wide_body
+    return plan(density, background, member_ids, layer_kernel, kernel_spectra)
+
+
 def solution(mesh):
     placed = (
         P(("grp", "mem"), "depth", "pencil", None),

time: 241 us -> 199 us (0.83); the launches traced: 236 us -> 198 us
  Pallas kernels: 41 us -> 195 us
  blocking collectives: 77.6 us -> 0 us
  waiting for transfers between devices: 73 us -> 0 us
  starting transfers between devices: 16.2 us -> 0 us
  between operations: 14.8 us -> 1.34 us
  other arithmetic: 7.62 us -> 0 us
  local copies, waits for them, and re-layouts: 6.04 us -> 2.17 us
    pallas_call x5 -> x2, Pallas kernels: 41 us -> 195 us  [the longest x1 193 us: fused_body(): pl.pallas_call(functools.partial(fused_kernel, pencils, depths), in_specs...]
    all_to_all x2 -> x0, blocking collectives: 77.6 us -> none  [the longest x1 51.7 us: body(): lax.all_to_all(part, 'pencil', 0, 0, tiled=True)]
    ppermute x4 -> x0, waiting for transfers between devices: 69.2 us -> none  [the longest x2 46.2 us: body(): before = out[0] + lax.ppermute(out[1], 'depth', [(0, 1), (1, 0)])]
    all_to_all x2 -> x0, starting transfers between devices: 13.9 us -> none  [the longest x1 7.48 us: body(): fields.append(lax.all_to_all(before, 'pencil', 0, 0, tiled=True))]
    all_to_all x2 -> x0, waiting for transfers between devices: 3.7 us -> none  [the longest x1 3.7 us: body(): lax.all_to_all(part, 'pencil', 0, 0, tiled=True)]
    unnamed x17 -> x4, local copies, waits for them, and re-layouts: 5.05 us -> 1.59 us
  transfers between devices with their start and end apart: 7 -> 0, of which waited for: 4 -> 0; matrix products, arithmetic and copies ran while one was open for 3% -> 0% of each run, Pallas kernels for 14% -> 0%
where the time goes in v2:
time: 199 us; the launch traced here: 198 us
  Pallas kernels  195 us (98%)
  local copies, waits for them, and re-layouts  2.17 us (1%)
    pallas_call x1, Pallas kernels, fused_body(): pl.pallas_call(functools.partial(fused_kernel, pencils, depths), in_specs...  193 us

profile of v2, /device:TPU:18, one launch (start us, length us, event | category | flops | bytes accessed | tf_op | source)
XLA Modules:
  0.0 198.2 jit_solution(13897710441568204613)
XLA Ops:
  0.0 0.0 copy-start
  1.3 0.0 copy-done
  1.3 0.6 constant_dynamic-slice_fusion
  1.9 192.7 %shard_map.145.pieces = f32[8,256,256]{2,1,0:T(8,128)} custom-call(f32[1]{0:T(128)} %bitcast.1.offset_ref, s32[1]{0:T(128)S(6)} %sub.7.local_ref, f32[4,16,2]{2,1,0:T(8,128)} %constant.33.clone.phase_ref, f32[1,1,512,2048]{3,2,1,0:T(8,128)} %density_ref.1, bf16[2,2,2048,512]{3,2,1,0:T(8,128)(2,1)} %kern_ref.1, ...), custom_call_target="tpu_custom_call" | custom-call | tf_op jit(solution)/shard_map/pallas_call | solution.py:922
  194.7 0.0 copy-start.1
  194.7 1.6 copy-done.1
  196.3 1.9 shard_map.146
Async XLA Ops:
  0.0 1.3 copy-start
  194.7 1.6 copy-start.1

commit v3 on v2

--- a/solution.py
+++ b/solution.py
@@ -397,10 +397,10 @@
 BLOCKS = 4
 
 
-def fused_kernel(pencils, depths, offset_ref, local_ref, phase_ref, density_ref, kern_ref, row_high_ref, row_low_ref,
+def fused_kernel(pencils, depths, background_ref, member_ref, layer_ref, phase_ref, density_ref, kern_ref, row_high_ref, row_low_ref,
                  back_high_ref, back_low_ref, table_ref, turns_ref, out_ref,
-                 dens, source, kern, row_high, row_low, back_high, back_low, tables, turns,
-                 pieces, sending, landing, moved, gathered, spectra, waves, keep, other_keep, fields,
+                 dens, sources, kern, row_high, row_low, back_high, back_low, tables, turns,
+                 pieces, sending, landing, moved, gathered, spectra, waves, keep, other_keep, fields, half,
                  local_sem, b_sem, g_sem, a_send_sem, a_recv_sem, x_sem, c_sem):
     per = RADIX // pencils
     chunks = per // 2
@@ -414,7 +414,7 @@
     grp, mem = lax.axis_index("grp"), lax.axis_index("mem")
     sharer = grp * 2 + mem
     first = sharer * share
-    local = local_ref[0]
+    local = jnp.clip(layer_ref[0] - deep * kern.shape[0], 0, kern.shape[0] - 1)
 
     def remote(src, dst, send, recv, **where):
         return pltpu.make_async_remote_copy(
@@ -434,51 +434,58 @@
         return copy
 
     source_loads = [
-        load(kern_ref.at[:, :, pl.ds(pl.multiple_of(lax.rem(RADIX - first - u, RADIX) * INNER, INNER), INNER)], source.at[u])
+        load(kern_ref.at[:, :, pl.ds(pl.multiple_of(lax.rem(RADIX - first - u, RADIX) * INNER, INNER), INNER)], sources[u])
         for u in range(share)
     ]
-    dens_loads = [load(density_ref.at[0, 0, pl.ds(i * block, block)], dens.at[pl.ds(i * block, block)]) for i in range(BLOCKS)]
-    row_loads = [load(row_high_ref, row_high), load(row_low_ref, row_low)]
-    late_loads = [load(table_ref, tables), load(turns_ref, turns), load(kern_ref, kern),
-                  load(back_high_ref, back_high), load(back_low_ref, back_low)]
-
     barrier = pltpu.get_barrier_semaphore()
     peers = [{"pencil": toward(shift)} for shift in range(1, pencils)]
     peers += [{"depth": 1 - deep}, {"grp": 1 - grp}, {"mem": 1 - mem}]
     for peer in peers:
         pl.semaphore_signal(barrier, inc=1, device_id=peer, device_id_type=pl.DeviceIdType.MESH)
 
-    for copy in source_loads:
-        copy.wait()
+    row_loads = [load(row_high_ref, row_high), load(row_low_ref, row_low)]
+    dens_loads = [load(density_ref.at[0, 0, pl.ds(i * block, block)], dens.at[pl.ds(i * block, block)]) for i in range(BLOCKS)]
+    partner = lax.rem(pencils - me, pencils)
+
+    def rest(u):
+        at = pl.ds(1, per - 1)
+        return remote(moved.at[at, u], gathered.at[sharer, at, u], b_sem.at[0, u], b_sem.at[1, u], pencil=pencils - 1 - me)
+
+    def zero(u):
+        return remote(moved.at[0, u], gathered.at[sharer, 0, u], b_sem.at[2, u], b_sem.at[3, u], pencil=partner)
+
+    def stay(u):
+        return pltpu.make_async_copy(moved.at[0, u], gathered.at[sharer, 0, u], b_sem.at[4, u])
+
     plain = swapped(me < 0, (INNER, HALF), 1)
     edge = swapped(me == 0, (INNER, HALF), 1)
     for u in range(share):
+        source_loads[u].wait()
         swap = swapped(first + u == 0, (INNER, INNER), 0)
-        rows = [dot(swap, source[u, local, c]).astype(bf16) for c in range(2)]
+        rows = [dot(swap, sources[u][local, c]).astype(bf16) for c in range(2)]
         for j in range(per):
             turn = edge if j == 0 else plain
             turned = [dot(rows[c][:, j * INNER : (j + 1) * INNER], turn) for c in range(2)]
             moved[(per - j) % per, u] = jnp.concatenate(turned, axis=1)
 
-    pl.semaphore_wait(barrier, len(peers))
-    rest = remote(moved.at[pl.ds(1, per - 1)], gathered.at[sharer, pl.ds(1, per - 1)], b_sem.at[0], b_sem.at[1],
-                  pencil=pencils - 1 - me)
-    rest.start()
-    partner = lax.rem(pencils - me, pencils)
-    zero = remote(moved.at[0], gathered.at[sharer, 0], b_sem.at[2], b_sem.at[3], pencil=partner)
-    stay = pltpu.make_async_copy(moved.at[0], gathered.at[sharer, 0], b_sem.at[4])
-
-    @pl.when(partner != me)
-    def _():
-        zero.start()
-
-    @pl.when(partner == me)
-    def _():
-        stay.start()
+        if u == 0:
+            pl.semaphore_wait(barrier, len(peers))
+        rest(u).start()
+
+        @pl.when(partner != me)
+        def _(u=u):
+            zero(u).start()
+
+        @pl.when(partner == me)
+        def _(u=u):
+            stay(u).start()
+
+    late_loads = [load(table_ref, tables), load(turns_ref, turns), load(kern_ref, kern),
+                  load(back_high_ref, back_high), load(back_low_ref, back_low)]
 
     for copy in row_loads:
         copy.wait()
-    offset = offset_ref[0]
+    offset = background_ref[member_ref[0]]
 
     def a_copy(chunk, shift, i):
         at = pl.ds(i * block, block)
@@ -520,28 +527,29 @@
             a_copy(0, shift, i).start()
 
     def start_a(chunk):
-        for shift in SHIFTS:
-            for i in range(BLOCKS):
+        for i in range(BLOCKS):
+            for shift in SHIFTS:
                 a_copy(chunk, shift, i).start()
 
-    def wait_a(chunk):
-        for shift in SHIFTS:
-            for i in range(BLOCKS):
+    def wait_a(chunk, blocks):
+        for i in blocks:
+            for shift in SHIFTS:
                 a_copy(chunk, shift, i).wait_recv()
 
     for copy in late_loads:
         copy.wait()
 
-    rest.wait_recv()
-
-    @pl.when(partner != me)
-    def _():
-        zero.wait_recv()
-        zero.wait_send()
-
-    @pl.when(partner == me)
-    def _():
-        stay.wait()
+    for u in range(share):
+        rest(u).wait_recv()
+
+        @pl.when(partner != me)
+        def _(u=u):
+            zero(u).wait_recv()
+            zero(u).wait_send()
+
+        @pl.when(partner == me)
+        def _(u=u):
+            stay(u).wait()
 
     own = gathered.at[sharer]
     far = (1 - grp) * 2 + mem
@@ -549,8 +557,8 @@
     across.start()
     beside = remote(own, own, g_sem.at[2], g_sem.at[3], mem=1 - mem)
     beside.start()
-    if not PACED:
-        start_a(1)
+    wait_a(0, range(AHEAD))
+    start_a(1)
     across.wait_recv()
     passed = remote(gathered.at[far], gathered.at[far], g_sem.at[4], g_sem.at[5], mem=1 - mem)
     passed.start()
@@ -664,51 +672,76 @@
         return remote(keep.at[chunk, 1, j], other_keep.at[chunk, j], x_sem.at[0, chunk, j], x_sem.at[1, chunk, j],
                       depth=1 - deep)
 
-    def c_copy(chunk, j):
-        return remote(keep.at[chunk, 0, j], fields.at[chunk, j - 1], c_sem.at[0, chunk, j - 1], c_sem.at[1, chunk, j - 1],
-                      pencil=toward(j))
+    out_block = out_rows // PARTS
+
+    def c_copy(chunk, j, i):
+        at = pl.ds(i * out_block, out_block)
+        return remote(keep.at[chunk, 0, j, :, at], fields.at[chunk, j - 1, :, at],
+                      c_sem.at[0, chunk, j - 1, i], c_sem.at[1, chunk, j - 1, i], pencil=toward(j))
+
+    def start_c(chunk, j):
+        if j:
+            for i in range(PARTS):
+                c_copy(chunk, j, i).start()
 
     def summed(chunk, j):
         x_copy(chunk, j).wait_recv()
         keep[chunk, 0, j] += other_keep[chunk, j]
 
-    def gather_field(chunk, shift):
+    def gather_field(chunk, shift, i):
         t = lax.rem(me + pencils - shift, pencils) * chunks + chunk
+        at = pl.ds(i * out_block, out_block)
         ref = keep.at[chunk, 0, 0] if shift == 0 else fields.at[chunk, shift - 1]
-        high, low = split_value(jnp.concatenate([ref[0], ref[1]], axis=1))
+        high, low = split_value(jnp.concatenate([ref[0, at], ref[1, at]], axis=1))
         for odd in range(2):
             r = 2 * t + odd
-            out_ref[slot_at(r)] += dot(high, back_high[r]) + dot(low, back_high[r]) + dot(high, back_low[r])
-
-    out_ref[...] = jnp.zeros_like(out_ref)
-    wait_a(0)
-    if PACED:
-        start_a(1)
+            half[slot_at(r), at] += dot(high, back_high[r]) + dot(low, back_high[r]) + dot(high, back_low[r])
+
+    def last(b, carry):
+        at = pl.ds(pl.multiple_of(b * 8, 8), 8)
+        values = [(half[0, at, :INNER], None)]
+        for s in range(1, 8):
+            values.append((half[s, at, :INNER], half[s, at, INNER:]))
+        values.append((half[0, at, INNER:], None))
+        for n, value in enumerate(real_inverse(values)):
+            out_ref[0, at, n * INNER : (n + 1) * INNER] = value
+        return carry
+
+    half[...] = jnp.zeros_like(half)
+    wait_a(0, range(AHEAD, BLOCKS))
     columns(0)
     for j in ORDER:
         x_copy(0, j).start()
     for j in ORDER:
         summed(0, j)
-    wait_a(1)
+    wait_a(1, range(BEFORE))
     for j in ORDER:
-        if j:
-            c_copy(0, j).start()
+        start_c(0, j)
+    wait_a(1, range(BEFORE, BLOCKS))
     columns(1)
     for j in ORDER:
         x_copy(1, j).start()
-    gather_field(0, 0)
+    for i in range(PARTS):
+        gather_field(0, 0, i)
     for j in ORDER:
         summed(1, j)
+        start_c(1, j)
+    for i in range(PARTS):
+        gather_field(1, 0, i)
+    for j in ORDER:
         if j:
-            c_copy(1, j).start()
-    gather_field(1, 0)
-    for chunk in range(chunks):
+            for i in range(PARTS):
+                c_copy(0, j, i).wait_recv()
+                gather_field(0, j, i)
+    for i in range(PARTS):
         for j in ORDER:
             if j:
-                c_copy(chunk, j).wait_recv()
-                gather_field(chunk, j)
-
-    rest.wait_send()
+                c_copy(1, j, i).wait_recv()
+                gather_field(1, j, i)
+        lax.fori_loop(i * out_block // 8, (i + 1) * out_block // 8, last, 0)
+
+    for u in range(share):
+        rest(u).wait_send()
     across.wait_send()
     beside.wait_send()
     passed.wait_send()
@@ -719,27 +752,16 @@
         for j in ORDER:
             x_copy(chunk, j).wait_send()
             if j:
-                c_copy(chunk, j).wait_send()
-
-
-def last_kernel(pieces, out_ref):
-    def step(b, carry):
-        at = pl.ds(pl.multiple_of(b * 8, 8), 8)
-        values = [(pieces[0, at, :INNER], None)]
-        for s in range(1, 8):
-            values.append((pieces[s, at, :INNER], pieces[s, at, INNER:]))
-        values.append((pieces[0, at, INNER:], None))
-        for n, value in enumerate(real_inverse(values)):
-            out_ref[0, at, n * INNER : (n + 1) * INNER] = value
-        return carry
-
-    lax.fori_loop(0, out_ref.shape[1] // 8, step, 0)
+                for i in range(PARTS):
+                    c_copy(chunk, j, i).wait_send()
 
 
 SHIFTS = (2, 1, 3)
 ORDER = (2, 1, 3, 0)
 UNROLL = 4
-PACED = True
+AHEAD = 3
+BEFORE = 4
+PARTS = 2
 
 
 def params(**more):
@@ -908,8 +930,6 @@
     anywhere = pl.BlockSpec(memory_space=pl.ANY)
     vmem = pl.BlockSpec(memory_space=pltpu.VMEM)
 
-    offset = lax.dynamic_index_in_dim(background[:, 0], member_ids[0], 0, keepdims=True)
-    local = layer_kernel - lax.axis_index("depth") * kernel_spectra.shape[0]
     angles = 2 * np.pi * np.arange(pencils)[:, None] * np.arange(RADIX)[None, :] / pencils
     phases = jnp.asarray(np.stack([np.cos(angles), np.sin(angles)], axis=-1).round(15), f32)
     row_high, row_low = halves(row_tables())
@@ -919,14 +939,14 @@
     tables = jnp.stack(halves(column) + halves(column.T))
     turns = jnp.asarray(turns)
     dma = pltpu.SemaphoreType.DMA
-    pieces = pl.pallas_call(
+    return pl.pallas_call(
         functools.partial(fused_kernel, pencils, depths),
-        in_specs=[smem] * 3 + [anywhere] * 8,
+        in_specs=[smem] * 4 + [anywhere] * 8,
         out_specs=vmem,
-        out_shape=jax.ShapeDtypeStruct((8, out_rows, 256), f32),
+        out_shape=jax.ShapeDtypeStruct((1, out_rows, LENGTH), f32),
         scratch_shapes=[
             pltpu.VMEM((part_rows, LENGTH), f32),
-            pltpu.VMEM((share, kernel_spectra.shape[0], 2, INNER, per * INNER), bf16),
+            [pltpu.VMEM((kernel_spectra.shape[0], 2, INNER, per * INNER), bf16)] * share,
             pltpu.VMEM(kernel_spectra.shape, bf16),
             pltpu.VMEM(row_high.shape, bf16),
             pltpu.VMEM(row_low.shape, bf16),
@@ -944,25 +964,19 @@
             pltpu.VMEM((chunks, 2, pencils, 2, out_rows, lanes), f32),
             pltpu.VMEM((chunks, pencils, 2, out_rows, lanes), f32),
             pltpu.VMEM((chunks, pencils - 1, 2, out_rows, lanes), f32),
+            pltpu.VMEM((8, out_rows, 256), f32),
             dma((share + BLOCKS + 7,)),
-            dma((5,)),
+            dma((5, share)),
             dma((6,)),
             dma((chunks, pencils - 1, BLOCKS)),
             dma((chunks, pencils - 1, BLOCKS)),
             dma((2, chunks, pencils)),
-            dma((2, chunks, pencils - 1)),
+            dma((2, chunks, pencils - 1, PARTS)),
         ],
         compiler_params=pltpu.CompilerParams(
             vmem_limit_bytes=60 * 1024 * 1024, collective_id=0, has_side_effects=True
         ),
-    )(offset, local, phases, density, kernel_spectra, row_high, row_low, back_high, back_low, tables, turns)
-    return pl.pallas_call(
-        last_kernel,
-        in_specs=[vmem],
-        out_specs=vmem,
-        out_shape=jax.ShapeDtypeStruct((1, out_rows, LENGTH), f32),
-        compiler_params=params(),
-    )(pieces)
+    )(background.reshape(-1), member_ids, layer_kernel, phases, density, kernel_spectra, row_high, row_low, back_high, back_low, tables, turns)
 
 
 def body(density, background, member_ids, layer_kernel, kernel_spectra):

time: 199 us -> 187 us (0.940)
  Pallas kernels: 195 us -> 182 us
    pallas_call x1, Pallas kernels: 193 us -> 182 us  [fused_body(): pl.pallas_call(functools.partial(fused_kernel, pencils, depths), in_specs...]
where the time goes in v3:
time: 187 us
  Pallas kernels  182 us (97%)
  local copies, waits for them, and re-layouts  3.14 us (2%)
    pallas_call x1, Pallas kernels, fused_body(): pl.pallas_call(functools.partial(fused_kernel, pencils, depths), in_specs...  182 us

profile of v3, /device:TPU:18, one launch (start us, length us, event | category | flops | bytes accessed | tf_op | source)
XLA Modules:
  0.0 186.8 jit_solution(1841300840624464683)
XLA Ops:
  1.3 182.4 %shard_map.145 = f32[1,256,2048]{2,1,0:T(8,128)} custom-call(f32[8]{0:T(128)} %bitcast.1, s32[1]{0:T(128)S(6)} %copy.17.member_ref, s32[1]{0:T(128)S(6)} %copy.18.layer_ref, f32[4,16,2]{2,1,0:T(8,128)} %constant.20.clone.phase_ref, f32[1,1,512,2048]{3,2,1,0:T(8,128)} %density_ref.1, bf16[2,2,2048,512]{3,2,1,0:T(8,128)(2,1)} %kern_ref.1, ...), custom_call_target="tpu_custom_call" | custom-call | tf_op jit(solution)/shard_map/pallas_call | solution.py:942
  183.7 3.1 %copy.19 = f32[1,256,2048]{2,1,0:T(8,128)} copy(f32[1,256,2048]{2,1,0:T(8,128)} %shard_map.145) | data formatting | bytes 4194304

commit v4 on v3

--- a/solution.py
+++ b/solution.py
@@ -408,7 +408,7 @@
     part_rows = dens.shape[0]
     block = part_rows // BLOCKS
     out_rows = part_rows // depths
-    share = moved.shape[1]
+    share = moved.shape[0]
     me = lax.axis_index("pencil")
     deep = lax.axis_index("depth")
     grp, mem = lax.axis_index("grp"), lax.axis_index("mem")
@@ -449,13 +449,13 @@
 
     def rest(u):
         at = pl.ds(1, per - 1)
-        return remote(moved.at[at, u], gathered.at[sharer, at, u], b_sem.at[0, u], b_sem.at[1, u], pencil=pencils - 1 - me)
+        return remote(moved.at[u, at], gathered.at[sharer, u, at], b_sem.at[0, u], b_sem.at[1, u], pencil=pencils - 1 - me)
 
     def zero(u):
-        return remote(moved.at[0, u], gathered.at[sharer, 0, u], b_sem.at[2, u], b_sem.at[3, u], pencil=partner)
+        return remote(moved.at[u, 0], gathered.at[sharer, u, 0], b_sem.at[2, u], b_sem.at[3, u], pencil=partner)
 
     def stay(u):
-        return pltpu.make_async_copy(moved.at[0, u], gathered.at[sharer, 0, u], b_sem.at[4, u])
+        return pltpu.make_async_copy(moved.at[u, 0], gathered.at[sharer, u, 0], b_sem.at[4, u])
 
     plain = swapped(me < 0, (INNER, HALF), 1)
     edge = swapped(me == 0, (INNER, HALF), 1)
@@ -466,7 +466,7 @@
         for j in range(per):
             turn = edge if j == 0 else plain
             turned = [dot(rows[c][:, j * INNER : (j + 1) * INNER], turn) for c in range(2)]
-            moved[(per - j) % per, u] = jnp.concatenate(turned, axis=1)
+            moved[u, (per - j) % per] = jnp.concatenate(turned, axis=1)
 
         if u == 0:
             pl.semaphore_wait(barrier, len(peers))
@@ -488,8 +488,7 @@
     offset = background_ref[member_ref[0]]
 
     def a_copy(chunk, shift, i):
-        at = pl.ds(i * block, block)
-        return remote(sending.at[chunk, shift, :, at], landing.at[chunk, shift - 1, :, at],
+        return remote(sending.at[chunk, shift, i], landing.at[chunk, shift - 1, i],
                       a_send_sem.at[chunk, shift - 1, i], a_recv_sem.at[chunk, shift - 1, i], pencil=toward(shift))
 
     for i in range(BLOCKS):
@@ -519,7 +518,7 @@
                 term = dot(high, table_high) + dot(low, table_high) + dot(high, table_low)
                 total = term if total is None else total + term
             for c in range(2):
-                sending[chunk, shift, c, i * block : (i + 1) * block] = total[:, c * 128 : (c + 1) * 128]
+                sending[chunk, shift, i, c] = total[:, c * 128 : (c + 1) * 128]
             return carry
 
         lax.fori_loop(0, pencils * chunks, part, 0)
@@ -531,10 +530,11 @@
             for shift in SHIFTS:
                 a_copy(chunk, shift, i).start()
 
-    def wait_a(chunk, blocks):
-        for i in blocks:
-            for shift in SHIFTS:
-                a_copy(chunk, shift, i).wait_recv()
+    arrivals = [(i, shift) for i in range(BLOCKS) for shift in SHIFTS]
+
+    def wait_a(chunk, which):
+        for i, shift in which:
+            a_copy(chunk, shift, i).wait_recv()
 
     for copy in late_loads:
         copy.wait()
@@ -557,7 +557,7 @@
     across.start()
     beside = remote(own, own, g_sem.at[2], g_sem.at[3], mem=1 - mem)
     beside.start()
-    wait_a(0, range(AHEAD))
+    wait_a(0, arrivals[:AHEAD])
     start_a(1)
     across.wait_recv()
     passed = remote(gathered.at[far], gathered.at[far], g_sem.at[4], g_sem.at[5], mem=1 - mem)
@@ -589,7 +589,7 @@
         holder, u = r // share, lax.rem(r, share)
         parts = []
         for c in range(2):
-            other = [gathered[holder, 2 * chunk + j, u, :, c * HALF : (c + 1) * HALF] for j in range(2)]
+            other = [gathered[holder, u, 2 * chunk + j, :, c * HALF : (c + 1) * HALF] for j in range(2)]
             other = jnp.concatenate(other, axis=1)
             mine = dot(kern[local, c, rows, 2 * chunk * INNER : 2 * (chunk + 1) * INNER], pick)
             parts.append(mine + 0.5 * other if c == 0 else mine - 0.5 * other)
@@ -626,8 +626,9 @@
             values = []
             for n in range(RADIX):
                 j, begin = divmod(n * INNER, part_rows)
+                i, begin = divmod(begin, block)
                 at = pl.ds(pl.multiple_of(begin + b * 8, 8), 8)
-                ref = sending.at[chunk, 0] if j == 0 else landing.at[chunk, pencils - j - 1]
+                ref = sending.at[chunk, 0, i] if j == 0 else landing.at[chunk, pencils - j - 1, i]
                 values.append((ref[0, at, :], ref[1, at, :]))
             at = pl.ds(pl.multiple_of(b * 8, 8), 8)
             also = pl.ds(pl.multiple_of(INNER + b * 8, 8), 8)
@@ -668,25 +669,22 @@
 
         lax.fori_loop(0, INNER // 8, backward, 0)
 
-    def x_copy(chunk, j):
-        return remote(keep.at[chunk, 1, j], other_keep.at[chunk, j], x_sem.at[0, chunk, j], x_sem.at[1, chunk, j],
-                      depth=1 - deep)
-
     out_block = out_rows // PARTS
+
+    def x_copy(chunk, j, i):
+        at = pl.ds(i * out_block, out_block)
+        return remote(keep.at[chunk, 1, j, :, at], other_keep.at[chunk, j, :, at],
+                      x_sem.at[0, chunk, j, i], x_sem.at[1, chunk, j, i], depth=1 - deep)
 
     def c_copy(chunk, j, i):
         at = pl.ds(i * out_block, out_block)
         return remote(keep.at[chunk, 0, j, :, at], fields.at[chunk, j - 1, :, at],
                       c_sem.at[0, chunk, j - 1, i], c_sem.at[1, chunk, j - 1, i], pencil=toward(j))
 
-    def start_c(chunk, j):
-        if j:
-            for i in range(PARTS):
-                c_copy(chunk, j, i).start()
-
-    def summed(chunk, j):
-        x_copy(chunk, j).wait_recv()
-        keep[chunk, 0, j] += other_keep[chunk, j]
+    def summed(chunk, j, i):
+        x_copy(chunk, j, i).wait_recv()
+        at = pl.ds(i * out_block, out_block)
+        keep[chunk, 0, j, :, at] += other_keep[chunk, j, :, at]
 
     def gather_field(chunk, shift, i):
         t = lax.rem(me + pencils - shift, pencils) * chunks + chunk
@@ -697,48 +695,45 @@
             r = 2 * t + odd
             half[slot_at(r), at] += dot(high, back_high[r]) + dot(low, back_high[r]) + dot(high, back_low[r])
 
-    def last(b, carry):
-        at = pl.ds(pl.multiple_of(b * 8, 8), 8)
-        values = [(half[0, at, :INNER], None)]
-        for s in range(1, 8):
-            values.append((half[s, at, :INNER], half[s, at, INNER:]))
-        values.append((half[0, at, INNER:], None))
-        for n, value in enumerate(real_inverse(values)):
-            out_ref[0, at, n * INNER : (n + 1) * INNER] = value
-        return carry
-
     half[...] = jnp.zeros_like(half)
-    wait_a(0, range(AHEAD, BLOCKS))
+    wait_a(0, arrivals[AHEAD:])
     columns(0)
-    for j in ORDER:
-        x_copy(0, j).start()
-    for j in ORDER:
-        summed(0, j)
-    wait_a(1, range(BEFORE))
-    for j in ORDER:
-        start_c(0, j)
-    wait_a(1, range(BEFORE, BLOCKS))
+    pairs = [(i, j) for i in range(PARTS) for j in ORDER]
+    for i, j in pairs:
+        x_copy(0, j, i).start()
+    for i, j in pairs:
+        summed(0, j, i)
+    wait_a(1, arrivals[:BEFORE])
+    for i, j in pairs:
+        if j:
+            c_copy(0, j, i).start()
+    wait_a(1, arrivals[BEFORE:])
     columns(1)
-    for j in ORDER:
-        x_copy(1, j).start()
+    for i, j in pairs:
+        x_copy(1, j, i).start()
     for i in range(PARTS):
         gather_field(0, 0, i)
-    for j in ORDER:
-        summed(1, j)
-        start_c(1, j)
+    for i, j in pairs:
+        summed(1, j, i)
+        if j:
+            c_copy(1, j, i).start()
     for i in range(PARTS):
         gather_field(1, 0, i)
-    for j in ORDER:
+    for i, j in pairs:
         if j:
-            for i in range(PARTS):
-                c_copy(0, j, i).wait_recv()
-                gather_field(0, j, i)
+            c_copy(0, j, i).wait_recv()
+            gather_field(0, j, i)
+    leaving = []
     for i in range(PARTS):
         for j in ORDER:
             if j:
                 c_copy(1, j, i).wait_recv()
                 gather_field(1, j, i)
-        lax.fori_loop(i * out_block // 8, (i + 1) * out_block // 8, last, 0)
+        at = pl.ds(i * out_block, out_block)
+        leaving.append(pltpu.make_async_copy(half.at[:, at], out_ref.at[:, at], local_sem.at[i]))
+        leaving[-1].start()
+    for copy in leaving:
+        copy.wait()
 
     for u in range(share):
         rest(u).wait_send()
@@ -750,18 +745,47 @@
             for i in range(BLOCKS):
                 a_copy(chunk, shift, i).wait_send()
         for j in ORDER:
-            x_copy(chunk, j).wait_send()
-            if j:
-                for i in range(PARTS):
+            for i in range(PARTS):
+                x_copy(chunk, j, i).wait_send()
+                if j:
                     c_copy(chunk, j, i).wait_send()
 
 
+def last_kernel(in_ref, out_ref, half, done, sem):
+    block = half.shape[1] // LAST
+
+    def copies(i):
+        at = pl.ds(i * block, block)
+        return (pltpu.make_async_copy(in_ref.at[:, at], half.at[:, at], sem.at[0, i]),
+                pltpu.make_async_copy(done.at[at], out_ref.at[0, at], sem.at[1, i]))
+
+    def last(b, carry):
+        at = pl.ds(pl.multiple_of(b * 8, 8), 8)
+        values = [(half[0, at, :INNER], None)]
+        for s in range(1, 8):
+            values.append((half[s, at, :INNER], half[s, at, INNER:]))
+        values.append((half[0, at, INNER:], None))
+        for n, value in enumerate(real_inverse(values)):
+            done[at, n * INNER : (n + 1) * INNER] = value
+        return carry
+
+    for i in range(LAST):
+        copies(i)[0].start()
+    for i in range(LAST):
+        copies(i)[0].wait()
+        lax.fori_loop(i * block // 8, (i + 1) * block // 8, last, 0)
+        copies(i)[1].start()
+    for i in range(LAST):
+        copies(i)[1].wait()
+
+
+LAST = 4
 SHIFTS = (2, 1, 3)
 ORDER = (2, 1, 3, 0)
 UNROLL = 4
-AHEAD = 3
-BEFORE = 4
-PARTS = 2
+AHEAD = 9
+BEFORE = 12
+PARTS = 1
 
 
 def params(**more):
@@ -928,7 +952,6 @@
     share = RADIX // sharers
     smem = pl.BlockSpec(memory_space=pltpu.SMEM)
     anywhere = pl.BlockSpec(memory_space=pl.ANY)
-    vmem = pl.BlockSpec(memory_space=pltpu.VMEM)
 
     angles = 2 * np.pi * np.arange(pencils)[:, None] * np.arange(RADIX)[None, :] / pencils
     phases = jnp.asarray(np.stack([np.cos(angles), np.sin(angles)], axis=-1).round(15), f32)
@@ -939,11 +962,11 @@
     tables = jnp.stack(halves(column) + halves(column.T))
     turns = jnp.asarray(turns)
     dma = pltpu.SemaphoreType.DMA
-    return pl.pallas_call(
+    half = pl.pallas_call(
         functools.partial(fused_kernel, pencils, depths),
         in_specs=[smem] * 4 + [anywhere] * 8,
-        out_specs=vmem,
-        out_shape=jax.ShapeDtypeStruct((1, out_rows, LENGTH), f32),
+        out_specs=anywhere,
+        out_shape=jax.ShapeDtypeStruct((8, out_rows, 256), f32),
         scratch_shapes=[
             pltpu.VMEM((part_rows, LENGTH), f32),
             [pltpu.VMEM((kernel_spectra.shape[0], 2, INNER, per * INNER), bf16)] * share,
@@ -955,10 +978,10 @@
             pltpu.VMEM(tables.shape, bf16),
             pltpu.VMEM(turns.shape, f32),
             pltpu.VMEM((8, part_rows // BLOCKS, 256), f32),
-            pltpu.VMEM((chunks, pencils, 2, part_rows, lanes), f32),
-            pltpu.VMEM((chunks, pencils - 1, 2, part_rows, lanes), f32),
-            pltpu.VMEM((per, share, INNER, INNER), f32),
-            pltpu.VMEM((sharers, per, share, INNER, INNER), f32),
+            pltpu.VMEM((chunks, pencils, BLOCKS, 2, part_rows // BLOCKS, lanes), f32),
+            pltpu.VMEM((chunks, pencils - 1, BLOCKS, 2, part_rows // BLOCKS, lanes), f32),
+            pltpu.VMEM((share, per, INNER, INNER), f32),
+            pltpu.VMEM((sharers, share, per, INNER, INNER), f32),
             pltpu.VMEM((RADIX, 256, lanes), f32),
             pltpu.VMEM((RADIX, 256, lanes), f32),
             pltpu.VMEM((chunks, 2, pencils, 2, out_rows, lanes), f32),
@@ -970,13 +993,25 @@
             dma((6,)),
             dma((chunks, pencils - 1, BLOCKS)),
             dma((chunks, pencils - 1, BLOCKS)),
-            dma((2, chunks, pencils)),
+            dma((2, chunks, pencils, PARTS)),
             dma((2, chunks, pencils - 1, PARTS)),
         ],
         compiler_params=pltpu.CompilerParams(
             vmem_limit_bytes=60 * 1024 * 1024, collective_id=0, has_side_effects=True
         ),
     )(background.reshape(-1), member_ids, layer_kernel, phases, density, kernel_spectra, row_high, row_low, back_high, back_low, tables, turns)
+    return pl.pallas_call(
+        last_kernel,
+        in_specs=[anywhere],
+        out_specs=anywhere,
+        out_shape=jax.ShapeDtypeStruct((1, out_rows, LENGTH), f32),
+        scratch_shapes=[
+            pltpu.VMEM((8, out_rows, 256), f32),
+            pltpu.VMEM((out_rows, LENGTH), f32),
+            dma((2, LAST)),
+        ],
+        compiler_params=pltpu.CompilerParams(vmem_limit_bytes=60 * 1024 * 1024),
+    )(half)
 
 
 def body(density, background, member_ids, layer_kernel, kernel_spectra):

time: 187 us -> 186 us (level)
  local copies, waits for them, and re-layouts: 3.14 us -> 0 us
  Pallas kernels: 182 us -> 185 us
    unnamed x1 -> x0, local copies, waits for them, and re-layouts: 3.14 us -> none
    pallas_call x0 -> x1, Pallas kernels: none -> 2.56 us  [fused_body(): pl.pallas_call(last_kernel, in_specs=[anywhere], out_specs=anywhere, out_...]
where the time goes in v4:
time: 186 us
  Pallas kernels  185 us (99%)
    pallas_call x1, Pallas kernels, fused_body(): pl.pallas_call(functools.partial(fused_kernel, pencils, depths), in_specs...  182 us

profile of v4, /device:TPU:18, one launch (start us, length us, event | category | flops | bytes accessed | tf_op | source)
XLA Modules:
  0.0 186.1 jit_solution(17557874674150846705)
XLA Ops:
  1.3 182.2 %shard_map.145.in_ref = f32[8,256,256]{2,1,0:T(8,128)} custom-call(f32[8]{0:T(128)} %bitcast.1, s32[1]{0:T(128)S(6)} %copy.16.member_ref, s32[1]{0:T(128)S(6)} %copy.17.layer_ref, f32[4,16,2]{2,1,0:T(8,128)} %constant.20.clone.phase_ref, f32[1,1,512,2048]{3,2,1,0:T(8,128)} %density_ref.1, bf16[2,2,2048,512]{3,2,1,0:T(8,128)(2,1)} %kern_ref.1, ...), custom_call_target="tpu_custom_call" | custom-call | tf_op jit(solution)/shard_map/pallas_call | solution.py:965
  183.5 2.6 %shard_map.146 = f32[1,256,2048]{2,1,0:T(8,128)} custom-call(f32[8,256,256]{2,1,0:T(8,128)} %shard_map.145.in_ref), custom_call_target="tpu_custom_call" | custom-call | tf_op jit(solution)/shard_map/pallas_call | solution.py:1003

commit v5 on v4

--- a/solution.py
+++ b/solution.py
@@ -573,9 +573,9 @@
     mask = (to_lane == 0) & (me == 0)
 
     def turned(r):
-        c, s = turns[r, :, 0:1], turns[r, :, 1:2]
-        pc, ps = phase_ref[me, r, 0], phase_ref[me, r, 1]
-        return c * pc - s * ps, s * pc + c * ps
+        cos, sin = turns[r, :, 0:1], turns[r, :, 1:2]
+        pc, ps = (phase_ref[(me * RADIX + r) * 2 + c] for c in range(2))
+        return cos * pc - sin * ps, sin * pc + cos * ps
 
     def wave(r):
         re, im = spectra[r, :INNER], spectra[r, INNER:]
@@ -729,9 +729,10 @@
             if j:
                 c_copy(1, j, i).wait_recv()
                 gather_field(1, j, i)
-        at = pl.ds(i * out_block, out_block)
-        leaving.append(pltpu.make_async_copy(half.at[:, at], out_ref.at[:, at], local_sem.at[i]))
-        leaving[-1].start()
+        for quarter in range(LEAVE):
+            at = pl.ds(i * out_block + quarter * (out_block // LEAVE), out_block // LEAVE)
+            leaving.append(pltpu.make_async_copy(half.at[:, at], out_ref.at[:, at], local_sem.at[len(leaving)]))
+            leaving[-1].start()
     for copy in leaving:
         copy.wait()
 
@@ -760,7 +761,7 @@
                 pltpu.make_async_copy(done.at[at], out_ref.at[0, at], sem.at[1, i]))
 
     def last(b, carry):
-        at = pl.ds(pl.multiple_of(b * 8, 8), 8)
+        at = pl.ds(pl.multiple_of(b * STEP, STEP), STEP)
         values = [(half[0, at, :INNER], None)]
         for s in range(1, 8):
             values.append((half[s, at, :INNER], half[s, at, INNER:]))
@@ -773,19 +774,21 @@
         copies(i)[0].start()
     for i in range(LAST):
         copies(i)[0].wait()
-        lax.fori_loop(i * block // 8, (i + 1) * block // 8, last, 0)
+        lax.fori_loop(i * block // STEP, (i + 1) * block // STEP, last, 0)
         copies(i)[1].start()
     for i in range(LAST):
         copies(i)[1].wait()
 
 
-LAST = 4
+STEP = 16
+LAST = 8
 SHIFTS = (2, 1, 3)
 ORDER = (2, 1, 3, 0)
 UNROLL = 4
 AHEAD = 9
 BEFORE = 12
 PARTS = 1
+LEAVE = 4
 
 
 def params(**more):
@@ -954,7 +957,7 @@
     anywhere = pl.BlockSpec(memory_space=pl.ANY)
 
     angles = 2 * np.pi * np.arange(pencils)[:, None] * np.arange(RADIX)[None, :] / pencils
-    phases = jnp.asarray(np.stack([np.cos(angles), np.sin(angles)], axis=-1).round(15), f32)
+    phases = jnp.asarray(np.stack([np.cos(angles), np.sin(angles)], axis=-1).round(15).reshape(-1), f32)
     row_high, row_low = halves(row_tables())
     where = [0 if r == 8 else min(r, RADIX - r) for r in range(RADIX)], [int(r >= 8) for r in range(RADIX)]
     back_high, back_low = halves(inverse_row_tables().reshape(8, 2, 256, 256)[where])

time: 186 us -> 186 us (level)
  no operation moved by 1% of the time
where the time goes in v5:
time: 186 us; the launch traced here: 185 us
  Pallas kernels  184 us (99%)
    pallas_call x1, Pallas kernels, fused_body(): pl.pallas_call(functools.partial(fused_kernel, pencils, depths), in_specs...  182 us

profile of v5, /device:TPU:18, one launch (start us, length us, event | category | flops | bytes accessed | tf_op | source)
XLA Modules:
  0.0 185.5 jit_solution(6915002017720438479)
XLA Ops:
  1.3 181.7 %shard_map.145.in_ref = f32[8,256,256]{2,1,0:T(8,128)} custom-call(f32[8]{0:T(128)} %bitcast.1, s32[1]{0:T(128)S(6)} %copy.16.member_ref, s32[1]{0:T(128)S(6)} %copy.17.layer_ref, f32[128]{0:T(128)} %constant.20.clone.phase_ref, f32[1,1,512,2048]{3,2,1,0:T(8,128)} %density_ref.1, bf16[2,2,2048,512]{3,2,1,0:T(8,128)(2,1)} %kern_ref.1, ...), custom_call_target="tpu_custom_call" | custom-call | tf_op jit(solution)/shard_map/pallas_call | solution.py:968
  183.0 2.5 %shard_map.146 = f32[1,256,2048]{2,1,0:T(8,128)} custom-call(f32[8,256,256]{2,1,0:T(8,128)} %shard_map.145.in_ref), custom_call_target="tpu_custom_call" | custom-call | tf_op jit(solution)/shard_map/pallas_call | solution.py:1006

commit v6 on v5

--- a/solution.py
+++ b/solution.py
@@ -686,9 +686,10 @@
         at = pl.ds(i * out_block, out_block)
         keep[chunk, 0, j, :, at] += other_keep[chunk, j, :, at]
 
-    def gather_field(chunk, shift, i):
+    def gather_field(chunk, shift, i, size=None):
         t = lax.rem(me + pencils - shift, pencils) * chunks + chunk
-        at = pl.ds(i * out_block, out_block)
+        size = size or out_block
+        at = pl.ds(i * size, size)
         ref = keep.at[chunk, 0, 0] if shift == 0 else fields.at[chunk, shift - 1]
         high, low = split_value(jnp.concatenate([ref[0, at], ref[1, at]], axis=1))
         for odd in range(2):
@@ -724,14 +725,17 @@
             c_copy(0, j, i).wait_recv()
             gather_field(0, j, i)
     leaving = []
+    *ahead, final = [j for j in ORDER if j]
     for i in range(PARTS):
-        for j in ORDER:
-            if j:
-                c_copy(1, j, i).wait_recv()
-                gather_field(1, j, i)
-        for quarter in range(LEAVE):
-            at = pl.ds(i * out_block + quarter * (out_block // LEAVE), out_block // LEAVE)
-            leaving.append(pltpu.make_async_copy(half.at[:, at], out_ref.at[:, at], local_sem.at[len(leaving)]))
+        for j in ahead:
+            c_copy(1, j, i).wait_recv()
+            gather_field(1, j, i)
+        c_copy(1, final, i).wait_recv()
+        size = out_block // LEAVE
+        for piece in range(i * LEAVE, (i + 1) * LEAVE):
+            gather_field(1, final, piece, size)
+            at = pl.ds(piece * size, size)
+            leaving.append(pltpu.make_async_copy(half.at[:, at], out_ref.at[:, at], local_sem.at[piece]))
             leaving[-1].start()
     for copy in leaving:
         copy.wait()
@@ -783,7 +787,7 @@
 STEP = 16
 LAST = 8
 SHIFTS = (2, 1, 3)
-ORDER = (2, 1, 3, 0)
+ORDER = (2, 1, 0, 3)
 UNROLL = 4
 AHEAD = 9
 BEFORE = 12

time: 186 us -> 186 us (level)
  no operation moved by 1% of the time
where the time goes in v6:
time: 186 us; the launch traced here: 185 us
  Pallas kernels  184 us (99%)
    pallas_call x1, Pallas kernels, fused_body(): pl.pallas_call(functools.partial(fused_kernel, pencils, depths), in_specs...  182 us

profile of v6, /device:TPU:18, one launch (start us, length us, event | category | flops | bytes accessed | tf_op | source)
XLA Modules:
  0.0 185.4 jit_solution(23023329864926411)
XLA Ops:
  1.3 181.6 %shard_map.145.in_ref = f32[8,256,256]{2,1,0:T(8,128)} custom-call(f32[8]{0:T(128)} %bitcast.1, s32[1]{0:T(128)S(6)} %copy.16.member_ref, s32[1]{0:T(128)S(6)} %copy.17.layer_ref, f32[128]{0:T(128)} %constant.20.clone.phase_ref, f32[1,1,512,2048]{3,2,1,0:T(8,128)} %density_ref.1, bf16[2,2,2048,512]{3,2,1,0:T(8,128)(2,1)} %kern_ref.1, ...), custom_call_target="tpu_custom_call" | custom-call | tf_op jit(solution)/shard_map/pallas_call | solution.py:972
  182.9 2.5 %shard_map.146 = f32[1,256,2048]{2,1,0:T(8,128)} custom-call(f32[8,256,256]{2,1,0:T(8,128)} %shard_map.145.in_ref), custom_call_target="tpu_custom_call" | custom-call | tf_op jit(solution)/shard_map/pallas_call | solution.py:1010
